TPU v7x, 32 devices: a whole 2x2x4 slice. The times are simulated.
32 devices in a mesh: dp: 8 (over z, y), mix: 4 (over x, core).
Axes of the slice: x: 2, y: 2, z: 4, core: 2. Of those that a mesh axis runs over, the one named last changes fastest.
Arguments:
- images_in: bfloat16 [384, 196, 384], P('dp', 'mix'), may hold values from -6 to 6
- out_grad: bfloat16 [384, 196, 384], P('dp', 'mix'), may hold values from -6 to 6
- slot_mask: int32 [384], P('dp'), may hold values from 0 to 1, as said below
- mix_gain: bfloat16 [2, 384], replicated, may hold values from 0.5 to 1.5
- mix_shift: bfloat16 [2, 384], replicated, may hold values from -3 to 3
- mix_scale: bfloat16 [2, 384], replicated, may hold values from 0.5 to 1.5
- mix_weight: bfloat16 [2, 196, 196], replicated, may hold values from -0.4375 to 0.4375
- mix_bias: bfloat16 [2, 196], replicated, may hold values from -3 to 3
- mlp_gain: bfloat16 [2, 384], replicated, may hold values from 0.5 to 1.5
- mlp_shift: bfloat16 [2, 384], replicated, may hold values from -3 to 3
- mlp_scale: bfloat16 [2, 384], replicated, may hold values from 0.5 to 1.5
- up_weight: bfloat16 [2, 384, 1536], replicated, may hold values from -0.3125 to 0.3125
- up_bias: bfloat16 [2, 1536], replicated, may hold values from -3 to 3
- down_weight: bfloat16 [2, 1536, 384], replicated, may hold values from -0.15625 to 0.15625
- down_bias: bfloat16 [2, 384], replicated, may hold values from -3 to 3
Outputs:
- output: bfloat16 [384, 196, 384], P('dp', 'mix')
- input_grad: float32 [384, 196, 384], P('dp', 'mix')
- mix_gain_grad: float32 [2, 384], P(None, 'mix')
- mix_shift_grad: float32 [2, 384], P(None, 'mix')
- mix_scale_grad: float32 [2, 384], P(None, 'mix')
- mix_weight_grad: float32 [2, 196, 196], P(None, 'mix')
- mix_bias_grad: float32 [2, 196], P(None, 'mix')
- mlp_gain_grad: float32 [2, 384], P(None, 'mix')
- mlp_shift_grad: float32 [2, 384], P(None, 'mix')
- mlp_scale_grad: float32 [2, 384], P(None, 'mix')
- up_weight_grad: float32 [2, 384, 1536], P(None, None, 'mix')
- up_bias_grad: float32 [2, 1536], P(None, 'mix')
- down_weight_grad: float32 [2, 1536, 384], P(None, 'mix')
- down_bias_grad: float32 [2, 384], P(None, 'mix')
Inputs may be any that keep to these rules, and one draw needn't show every extreme that they name: `slot_mask`: 1 marks a filled slot, 0 an empty one. Each aligned group of 48 slots (those of one index of dp) holds between 36 and 48 filled slots at any positions; in every draw some group is full and some holds exactly 36.
All inputs are finite; a program needn't handle non-finite values.
Results may differ from a plain program's by a relative error of at most 0.013.
Values may be sent and summed in bfloat16 or wider, within the bound.
A program may use at most 192 MiB of HBM per device.

v0:
```python
import jax
import jax.numpy as jnp
from jax import lax
from jax.sharding import PartitionSpec as P


def mix_across(stream, gain_terms, mix_matrix, mix_offset):
    mixed_in = (gain_terms[0] * stream + gain_terms[1]).astype(jnp.bfloat16)
    across = jnp.einsum("pq,gqc->gpc", mix_matrix, mixed_in, preferred_element_type=jnp.float32)
    return (mixed_in, across + mix_offset[:, None])


def mlp_apply(patch_rows, gain_terms, weights):
    norm_gain, norm_shift, branch_scale = gain_terms
    up_matrix, up_offset, down_matrix, down_offset = weights
    row_values = patch_rows.astype(jnp.float32)
    normed = (norm_gain * row_values + norm_shift).astype(jnp.bfloat16)
    hidden = (
        jnp.einsum("gpc,ch->gph", normed, up_matrix, preferred_element_type=jnp.float32) + up_offset
    )
    active = jax.nn.gelu(hidden).astype(jnp.bfloat16)
    branch = (
        jnp.einsum("gph,hc->gpc", active, down_matrix, preferred_element_type=jnp.float32)
        + down_offset
    )
    return (row_values + branch_scale * branch).astype(jnp.bfloat16)


def mlp_backward(row_inputs, incoming, gain_terms, weights):
    norm_gain, norm_shift, branch_scale = gain_terms
    up_matrix, up_offset, down_matrix, down_offset = weights
    channels = row_inputs.shape[-1]
    row_values = row_inputs.reshape(-1, channels).astype(jnp.float32)
    upstream = incoming.reshape(-1, channels).astype(jnp.float32)
    normed = (norm_gain * row_values + norm_shift).astype(jnp.bfloat16)
    hidden = jnp.dot(normed, up_matrix, preferred_element_type=jnp.float32) + up_offset
    active_full, gelu_pull = jax.vjp(jax.nn.gelu, hidden)
    active = active_full.astype(jnp.bfloat16)
    branch = jnp.dot(active, down_matrix, preferred_element_type=jnp.float32) + down_offset
    scale_grad = jnp.sum(upstream * branch, axis=0)
    branch_grad = (branch_scale * upstream).astype(jnp.bfloat16)
    lower_bias = jnp.sum(branch_grad.astype(jnp.float32), axis=0)
    lower_weight = jnp.einsum("th,tc->hc", active, branch_grad, preferred_element_type=jnp.float32)
    active_grad = jnp.einsum(
        "tc,hc->th", branch_grad, down_matrix, preferred_element_type=jnp.float32
    )
    hidden_grad = gelu_pull(active_grad)[0].astype(jnp.bfloat16)
    upper_bias = jnp.sum(hidden_grad.astype(jnp.float32), axis=0)
    upper_weight = jnp.einsum("tc,th->ch", normed, hidden_grad, preferred_element_type=jnp.float32)
    normed_grad = jnp.einsum(
        "th,ch->tc", hidden_grad, up_matrix, preferred_element_type=jnp.float32
    )
    gain_grad = jnp.sum(normed_grad * row_values, axis=0)
    shift_grad = jnp.sum(normed_grad, axis=0)
    row_grad = upstream + norm_gain * normed_grad
    return (
        row_grad.reshape(incoming.shape),
        (gain_grad, shift_grad, scale_grad, upper_weight, upper_bias, lower_weight, lower_bias),
    )


def mix_backward(stream, incoming, gain_terms, mix_matrix, mix_offset):
    mixed_in, across = mix_across(stream, gain_terms, mix_matrix, mix_offset)
    scale_grad = jnp.sum(incoming * across, axis=(0, 1))
    across_grad = (gain_terms[2] * incoming).astype(jnp.bfloat16)
    bias_grad = jnp.sum(across_grad.astype(jnp.float32), axis=(0, 2))
    weight_grad = jnp.einsum(
        "gpc,gqc->pq", across_grad, mixed_in, preferred_element_type=jnp.float32
    )
    mixed_grad = jnp.einsum(
        "pq,gpc->gqc", mix_matrix, across_grad, preferred_element_type=jnp.float32
    )
    gain_grad = jnp.sum(mixed_grad * stream, axis=(0, 1))
    shift_grad = jnp.sum(mixed_grad, axis=(0, 1))
    carried = incoming + gain_terms[0] * mixed_grad
    return (carried, (gain_grad, shift_grad, scale_grad, weight_grad, bias_grad))


def reduce_grads(mix_part, mlp_part):
    members = tuple(mix_part) + tuple(mlp_part)
    summed = lax.psum(
        (
            members[0],
            members[1],
            members[2],
            members[3],
            members[4],
            members[5],
            members[6],
            members[7],
            members[8],
            members[9],
            members[10],
            members[11],
        ),
        "dp",
    )
    return tuple(
        (
            lax.psum_scatter(summed[0], "mix", scatter_dimension=0, tiled=True),
            lax.psum_scatter(summed[1], "mix", scatter_dimension=0, tiled=True),
            lax.psum_scatter(summed[2], "mix", scatter_dimension=0, tiled=True),
            lax.psum_scatter(summed[3], "mix", scatter_dimension=0, tiled=True),
            lax.psum_scatter(summed[4], "mix", scatter_dimension=0, tiled=True),
            lax.psum_scatter(summed[5], "mix", scatter_dimension=0, tiled=True),
            lax.psum_scatter(summed[6], "mix", scatter_dimension=0, tiled=True),
            lax.psum_scatter(summed[7], "mix", scatter_dimension=0, tiled=True),
            lax.psum_scatter(summed[8], "mix", scatter_dimension=1, tiled=True),
            lax.psum_scatter(summed[9], "mix", scatter_dimension=0, tiled=True),
            lax.psum_scatter(summed[10], "mix", scatter_dimension=0, tiled=True),
            lax.psum_scatter(summed[11], "mix", scatter_dimension=0, tiled=True),
        )
    )


def local(
    images_in,
    out_grad,
    slot_mask,
    mix_gain,
    mix_shift,
    mix_scale,
    mix_weight,
    mix_bias,
    mlp_gain,
    mlp_shift,
    mlp_scale,
    up_weight,
    up_bias,
    down_weight,
    down_bias,
):
    layer_count = up_weight.shape[0]

    def first_terms(layer_index):
        return (
            mix_gain[layer_index].astype(jnp.float32),
            mix_shift[layer_index].astype(jnp.float32),
            mix_scale[layer_index].astype(jnp.float32),
        )

    def second_terms(layer_index):
        return (
            mlp_gain[layer_index].astype(jnp.float32),
            mlp_shift[layer_index].astype(jnp.float32),
            mlp_scale[layer_index].astype(jnp.float32),
        )

    def mlp_terms(layer_index):
        return (
            up_weight[layer_index],
            up_bias[layer_index].astype(jnp.float32),
            down_weight[layer_index],
            down_bias[layer_index].astype(jnp.float32),
        )

    stream = images_in.astype(jnp.float32)
    image_inputs = []
    kept_rows = []
    for layer_index in range(layer_count):
        whole = lax.all_to_all(
            stream.astype(jnp.bfloat16), "mix", split_axis=0, concat_axis=1, tiled=True
        )
        image_inputs.append(whole)
        image_stream = whole.astype(jnp.float32)
        gain_terms = first_terms(layer_index)
        mixed_in, across = mix_across(
            image_stream,
            gain_terms,
            mix_weight[layer_index],
            mix_bias[layer_index].astype(jnp.float32),
        )
        mixed_out = (image_stream + gain_terms[2] * across).astype(jnp.bfloat16)
        first_rows = lax.all_to_all(mixed_out, "mix", split_axis=1, concat_axis=0, tiled=True)
        kept_rows.append(first_rows)
        stream = mlp_apply(first_rows, second_terms(layer_index), mlp_terms(layer_index)).astype(
            jnp.float32
        )
    slot_weight = slot_mask.astype(jnp.float32)[:, None, None]
    output = (slot_weight * stream).astype(jnp.bfloat16)
    carried = slot_weight * out_grad.astype(jnp.float32)
    per_layer = [None] * layer_count
    for layer_index in reversed(range(layer_count)):
        row_grad, mlp_part = mlp_backward(
            kept_rows[layer_index],
            carried.astype(jnp.bfloat16),
            second_terms(layer_index),
            mlp_terms(layer_index),
        )
        first_grad = lax.all_to_all(
            row_grad.astype(jnp.bfloat16), "mix", split_axis=0, concat_axis=1, tiled=True
        ).astype(jnp.float32)
        image_carried, mix_part = mix_backward(
            image_inputs[layer_index].astype(jnp.float32),
            first_grad,
            first_terms(layer_index),
            mix_weight[layer_index],
            mix_bias[layer_index].astype(jnp.float32),
        )
        carried = lax.all_to_all(image_carried, "mix", split_axis=1, concat_axis=0, tiled=True)
        per_layer[layer_index] = reduce_grads(mix_part, mlp_part)
    stacked = tuple(
        (
            jnp.stack([per_layer[level_index][member] for level_index in range(layer_count)])
            for member in range(12)
        )
    )
    return (output, carried) + stacked


def solution(mesh):
    in_specs = (
        P("dp", "mix", None),
        P("dp", "mix", None),
        P("dp"),
        P(),
        P(),
        P(),
        P(),
        P(),
        P(),
        P(),
        P(),
        P(),
        P(),
        P(),
        P(),
    )
    out_specs = (
        P("dp", "mix", None),
        P("dp", "mix", None),
        P(None, "mix"),
        P(None, "mix"),
        P(None, "mix"),
        P(None, "mix", None),
        P(None, "mix"),
        P(None, "mix"),
        P(None, "mix"),
        P(None, "mix"),
        P(None, None, "mix"),
        P(None, "mix"),
        P(None, "mix", None),
        P(None, "mix"),
    )
    return jax.shard_map(local, mesh=mesh, in_specs=in_specs, out_specs=out_specs, check_vma=False)
```

profile of v0, /device:TPU:0, one launch (start us, length us, event | category | flops | bytes accessed | tf_op | source)
XLA Modules:
  0.0 743.6 jit_solution(6259052541567080813)
XLA Ops:
  8.1 3.3 copy.138
  11.3 4.2 all-to-all-start
  16.0 24.9 %all-to-all-done = bf16[48,49,384]{2,1,0:T(8,128)(2,1)S(1)} async-done(((bf16[48,49,384]{2,1,0:T(8,128)(2,1)}), bf16[48,49,384]{2,1,0:T(8,128)(2,1)S(1)}, u32[]{:S(2)}, u32[]{:S(2)}) %all-to-all-start) | async-done | bytes 1806368 | tf_op jit(solution)/shard_map/all_to_all | solution.py:161
  45.9 4.5 copy.139
  50.4 5.2 reshape.277
  55.6 4.6 fusion.56
  62.0 3.6 all-to-all-start.1
  66.4 28.2 %all-to-all-done.1 = bf16[12,196,384]{2,0,1:T(8,128)(2,1)S(1)} async-done(((bf16[12,196,384]{2,0,1:T(8,128)(2,1)}), bf16[12,196,384]{2,0,1:T(8,128)(2,1)S(1)}, u32[]{:S(2)}, u32[]{:S(2)}) %all-to-all-start.1) | async-done | bytes 1806368 | tf_op jit(solution)/shard_map/all_to_all | solution.py:174
  96.9 4.9 reshape.313
  101.8 2.7 fusion.58
  107.4 15.4 %fusion.43 = bf16[48,49,384]{2,1,0:T(8,128)(2,1)} fusion(f32[4,12,49,384]{3,2,1,0:T(8,128)} %copy.144, f32[384]{0:T(512)S(1)} %get-tuple-element.97, f32[384]{0:T(512)S(1)} %get-tuple-element.187, f32[1536]{0:T(1024)S(1)} %get-tuple-element.89, bf16[48,49,384]{2,1,0:T(8,128)(2,1)S(1)} %bitcast.209, bf16[2,1536,384]{2,1,0:T(8,128)(2,1)} %param.28, ...), kind=kOutput, calls=%fused_computation.61 | convolution fusion | flops 5588803584 | bytes 10109952 | tf_op jit(solution)/shard_map/gph,hc->gpc/dot_general | solution.py:23
  122.8 29.4 %all_to_all.81 = bf16[48,49,384]{2,1,0:T(8,128)(2,1)S(1)} all-to-all(bf16[48,49,384]{2,1,0:T(8,128)(2,1)} %fusion.43), channel_id=1, replica_groups=mesh['dp'=8,'mix'=4] {'mix'}, dimensions={0} | all-to-all | bytes 3612672 | tf_op jit(solution)/shard_map/all_to_all | solution.py:161
  156.8 5.2 reshape.288
  161.9 4.7 fusion.53
  168.4 3.6 all-to-all-start.3
  172.1 5.7 convert_reduce_fusion.2
  177.8 3.8 convert_element_type.603
  181.6 5.1 reshape.299
  186.7 14.4 %all-to-all-done.3 = bf16[12,196,384]{2,0,1:T(8,128)(2,1)S(1)} async-done(((bf16[12,196,384]{2,0,1:T(8,128)(2,1)}), bf16[12,196,384]{2,0,1:T(8,128)(2,1)S(1)}, u32[]{:S(2)}, u32[]{:S(2)}) %all-to-all-start.3) | async-done | bytes 1806368 | tf_op jit(solution)/shard_map/all_to_all | solution.py:174
  203.2 4.9 reshape.315
  213.1 4.4 copy.151
  217.5 5.0 reshape.304
  222.5 11.0 %convolution_add_fusion.1 = f32[2352,1536]{1,0:T(8,128)} fusion(bf16[2352,384]{1,0:T(8,128)(2,1)} %convert_element_type.604, f32[1536]{0:T(1024)S(1)} %get-tuple-element.88, bf16[2,384,1536]{2,1,0:T(8,128)(2,1)} %param.26), kind=kOutput, calls=%fused_computation.41 | convolution fusion | flops 2778144768 | bytes 17442816 | tf_op jit(solution)/shard_map/dot_general | solution.py:36
  233.6 16.8 %convert_reduce_fusion = (f32[1536]{0:T(1024)}, bf16[2352,1536]{1,0:T(8,128)(2,1)S(1)}) fusion(f32[2352,1536]{1,0:T(8,128)} %convolution_add_fusion.1, bf16[2352,384]{1,0:T(8,128)(2,1)S(1)} %copy-done.17, bf16[2,1536,384]{2,1,0:T(8,128)(2,1)S(1)} %copy-done.60), kind=kOutput, calls=%fused_computation.36 | convolution fusion | flops 2854009344 | bytes 24668160 | tf_op jit(solution)/shard_map/tc,hc->th/dot_general | solution.py:44
  250.4 7.3 fusion.136
  259.9 3.6 all-to-all-start.4
  263.6 8.9 %fusion.76 = f32[384,1536]{1,0:T(8,128)} fusion(bf16[2352,1536]{1,0:T(8,128)(2,1)} %copy-done.7, f32[2352,384]{1,0:T(8,128)} %reshape.304, f32[384]{0:T(512)S(1)} %get-tuple-element.92, f32[384]{0:T(512)S(1)} %get-tuple-element.186), kind=kOutput, calls=%fused_computation.127 | convolution fusion | flops 2777241600 | bytes 13200384 | tf_op jit(solution)/shard_map/tc,th->ch/dot_general | solution.py:49
  275.7 3.9 convert_element_type.623
  279.5 9.3 %all-to-all-done.4 = bf16[48,49,384]{2,1,0:T(8,128)(2,1)S(1)} async-done(((bf16[48,49,384]{2,1,0:T(8,128)(2,1)}), bf16[48,49,384]{2,1,0:T(8,128)(2,1)S(1)}, u32[]{:S(2)}, u32[]{:S(2)}) %all-to-all-start.4) | async-done | bytes 1806368 | tf_op jit(solution)/shard_map/all_to_all | solution.py:190
  291.0 3.9 convert_element_type.615
  297.5 5.2 reshape.300
  302.7 4.6 fusion.50
  309.1 3.6 all-to-all-start.5
  312.8 11.0 %fusion.78 = f32[1536,384]{1,0:T(8,128)} fusion(f32[2352,384]{1,0:T(8,128)} %reshape.299, f32[384]{0:T(512)S(1)} %get-tuple-element.188, f32[2352,1536]{1,0:T(8,128)} %convolution_add_fusion.1), kind=kOutput, calls=%fused_computation.129 | convolution fusion | flops 2808852480 | bytes 20424192 | tf_op jit(solution)/shard_map/th,tc->hc/dot_general | solution.py:43
  323.8 11.6 %convolution_add_fusion = f32[2352,1536]{1,0:T(8,128)} fusion(bf16[2352,384]{1,0:T(8,128)(2,1)} %convert_element_type.623, f32[1536]{0:T(1024)S(1)} %get-tuple-element.89, bf16[2,384,1536]{2,1,0:T(8,128)(2,1)} %param.26), kind=kOutput, calls=%fused_computation.40 | convolution fusion | flops 2778144768 | bytes 17442816 | tf_op jit(solution)/shard_map/dot_general | solution.py:36
  335.4 5.5 reshape.303
  343.9 5.0 reshape.317
  348.9 2.9 convert_reduce_fusion.3
  354.0 16.2 %convert_reduce_fusion.1 = (f32[1536]{0:T(1024)S(1)}, bf16[2352,1536]{1,0:T(8,128)(2,1)S(1)}) fusion(f32[2352,1536]{1,0:T(8,128)} %convolution_add_fusion, bf16[2352,384]{1,0:T(8,128)(2,1)} %convert_element_type.622, bf16[2,1536,384]{2,1,0:T(8,128)(2,1)} %param.28), kind=kOutput, calls=%fused_computation.37 | convolution fusion | flops 2854009344 | bytes 24668160 | tf_op jit(solution)/shard_map/tc,hc->th/dot_general | solution.py:44
  370.2 2.9 copy-done.6
  373.2 4.7 fusion.75
  378.0 9.4 %fusion.90 = f32[384]{0:T(512)S(1)} fusion(f32[2352,384]{1,0:T(8,128)} %reshape.299, f32[384]{0:T(512)S(1)} %copy-done.52, bf16[2,1536,384]{2,1,0:T(8,128)(2,1)} %param.28, f32[2352,1536]{1,0:T(8,128)} %convolution_add_fusion.1), kind=kOutput, calls=%fused_computation.137 | convolution fusion | flops 2809755136 | bytes 19246080 | tf_op jit(solution)/shard_map/dot_general | solution.py:39
  387.5 2.7 reduce_sum.169
  390.2 3.7 fusion.51
  402.2 5.1 reshape.301
  407.3 10.8 %fusion.77 = f32[1536,384]{1,0:T(8,128)} fusion(f32[2352,384]{1,0:T(8,128)} %reshape.301, f32[384]{0:T(512)S(1)} %get-tuple-element.187, f32[2352,1536]{1,0:T(8,128)} %convolution_add_fusion), kind=kOutput, calls=%fused_computation.128 | convolution fusion | flops 2808852480 | bytes 20424192 | tf_op jit(solution)/shard_map/th,tc->hc/dot_general | solution.py:43
  418.1 9.7 %fusion.135 = (f32[384]{0:T(512)S(1)}, f32[384]{0:T(512)S(1)}, bf16[2352,384]{1,0:T(8,128)(2,1)S(1)}) fusion(f32[2352,384]{1,0:T(8,128)} %reshape.303, f32[2352,384]{1,0:T(8,128)} %reshape.301, f32[384]{0:T(512)S(1)} %copy-done.24, bf16[2352,1536]{1,0:T(8,128)(2,1)} %copy-done.6, bf16[2,384,1536]{2,1,0:T(8,128)(2,1)} %param.26), kind=kOutput, calls=%fused_computation.212 | convolution fusion | flops 2779950080 | bytes 17441280 | tf_op jit(solution)/shard_map/th,ch->tc/dot_general | solution.py:50
  430.1 3.6 all-to-all-start.6
  433.8 9.6 %fusion.89 = f32[384]{0:T(512)S(1)} fusion(f32[2352,384]{1,0:T(8,128)} %reshape.301, f32[384]{0:T(512)S(1)} %copy-done.56, bf16[2,1536,384]{2,1,0:T(8,128)(2,1)} %param.28, f32[2352,1536]{1,0:T(8,128)} %convolution_add_fusion), kind=kOutput, calls=%fused_computation.136 | convolution fusion | flops 2809755136 | bytes 19246080 | tf_op jit(solution)/shard_map/dot_general | solution.py:39
  443.4 28.3 %all-to-all-done.6 = bf16[48,49,384]{2,1,0:T(8,128)(2,1)S(1)} async-done(((bf16[48,49,384]{2,1,0:T(8,128)(2,1)}), bf16[48,49,384]{2,1,0:T(8,128)(2,1)S(1)}, u32[]{:S(2)}, u32[]{:S(2)}) %all-to-all-start.6) | async-done | bytes 1806368 | tf_op jit(solution)/shard_map/all_to_all | solution.py:190
  473.8 3.9 convert_element_type.634
  480.3 5.1 reshape.302
  485.4 4.0 fusion.108
  489.5 9.2 %fusion.137 = (f32[56,196]{1,0:T(8,128)S(1)}, f32[56,196]{1,0:T(8,128)S(1)}) fusion(f32[196,196]{1,0:T(8,128)S(1)} %fusion.107, f32[196,196]{1,0:T(8,128)S(1)} %fusion.108), kind=kCustom, calls=%all-reduce-scatter.2 | all-reduce-scatter fusion | flops 87809 | bytes 395648
  500.0 3.9 collective-permute-start.1
  504.0 8.7 %fusion.57 = (f32[384]{0:T(512)S(1)}, f32[12,196,384]{2,1,0:T(8,128)}, f32[384]{0:T(512)S(1)}, f32[12,384,196]{1,2,0:T(8,128)}) fusion(f32[12,196,384]{2,1,0:T(8,128)} %reshape.302, f32[12,384,196]{1,2,0:T(8,128)} %get-tuple-element.173, f32[196]{0:T(256)S(1)} %bitcast.217, f32[384]{0:T(512)S(1)} %copy-done.28, f32[12,196,384]{2,1,0:T(8,128)} %reshape.277, ...), kind=kOutput, calls=%fused_computation.93 | convolution fusion | flops 360363264 | bytes 19951920 | tf_op jit(solution)/shard_map/pq,gpc->gqc/dot_general | solution.py:70
  515.2 10.6 %all-reduce.24 = (f32[384]{0:T(512)S(1)}, f32[384]{0:T(512)S(1)}, f32[384]{0:T(512)S(1)}, f32[384]{0:T(512)S(1)}, f32[384]{0:T(512)S(1)}, /*index=5*/f32[384]{0:...) all-reduce(f32[384]{0:T(512)S(1)} %fusion.51, ...), channel_id=3, replica_groups=mesh['dp'=8,'mix'=4] {'mix'}, use_global_device_ids=true, to_apply=%region_5.0.clone | all-reduce | flops 8840 | bytes 70720
  538.5 5.0 copy.166
  543.5 5.2 all-to-all-start.7
  549.3 15.8 %multiply_convert_fusion.5 = bf16[48,49,384]{2,1,0:T(8,128)(2,1)} fusion(f32[4,12,49,384]{3,2,1,0:T(8,128)} %copy.151, f32[384]{0:T(512)S(1)} %copy-done.52, f32[384]{0:T(512)S(1)} %copy-done.39, f32[48]{0:T(128)S(1)} %copy-done.59, f32[1536]{0:T(1024)S(1)} %copy-done.42, bf16[48,49,384]{2,1,0:T(8,128)(2,1)S(1)} %bitcast.208, ...), kind=kOutput, calls=%fused_computation.69 | convolution fusion | flops 5591513088 | bytes 10110144 | tf_op jit(solution)/shard_map/gph,hc->gpc/dot_general | solution.py:23
  565.1 3.0 copy.171
  568.1 49.3 %all-reduce.29.cloned.1.call-done = (f32[96]{0:T(128)}, f32[96]{0:T(128)}, f32[96]{0:T(128)}, f32[96]{0:T(128)}, f32[96]{0:T(128)}, /*index=5*/f32[96]{0:T(128)}...) async-done(((f32[96]{0:T(128)}, f32[96]{0:T(128)}, ...) | async-done | bytes 85688 | tf_op jit(solution)/shard_map/psum | solution.py:81
  630.7 3.5 copy.168
  636.7 94.7 %all-reduce.31.cloned.1.call-done = (f32[384,384]{1,0:T(8,128)}, f32[384,384]{1,0:T(8,128)}, f32[384,384]{1,0:T(8,128)}, f32[384,384]{1,0:T(8,128)}) async-done(((f32[384,384]{1,0:T(8,128)}, f32[384,384]{1,0:T(8,128)}, f32[384,384]{1,0:T(8,128)}, f32[384,384]{1,0:T(8,128)}), (f32[384,384]{1,0:T(8,128)}, f32[384,384]{1,0:T(8,128)}, f32[384,384]{1,0:T(8,128)}, ...) | async-done | bytes 2359312 | tf_op jit(solution)/shard_map/psum | solution.py:81
  (228 shorter events, 94.2 us)
Async XLA Ops:
  8.0 7.5 %copy-start.44 = (bf16[2,384]{1,0:T(2,128)(2,1)S(1)}, bf16[2,384]{1,0:T(2,128)(2,1)}, u32[]{:S(2)}) copy-start(bf16[2,384]{1,0:T(2,128)(2,1)} %param.20) | copy-start | bytes 4612
  8.0 7.5 %copy-start.45 = (bf16[2,384]{1,0:T(2,128)(2,1)S(1)}, bf16[2,384]{1,0:T(2,128)(2,1)}, u32[]{:S(2)}) copy-start(bf16[2,384]{1,0:T(2,128)(2,1)} %param.19) | copy-start | bytes 4612
  8.0 7.5 %copy-start.46 = (bf16[2,384]{1,0:T(2,128)(2,1)S(1)}, bf16[2,384]{1,0:T(2,128)(2,1)}, u32[]{:S(2)}) copy-start(bf16[2,384]{1,0:T(2,128)(2,1)} %param.18) | copy-start | bytes 4612
  8.0 7.6 %copy-start.51 = (bf16[2,196]{1,0:T(2,128)(2,1)S(1)}, bf16[2,196]{1,0:T(2,128)(2,1)}, u32[]{:S(2)}) copy-start(bf16[2,196]{1,0:T(2,128)(2,1)} %param.22) | copy-start | bytes 2356
  8.1 7.6 %copy-start.20 = (bf16[2,196,196]{2,0,1:T(2,128)(2,1)S(1)}, bf16[2,196,196]{2,0,1:T(2,128)(2,1)}, u32[]{:S(2)}) copy-start(bf16[2,196,196]{2,0,1:T(2,128)(2,1)} %param.21) | copy-start | bytes 460996
  11.3 29.6 %all-to-all-start = ((bf16[48,49,384]{2,1,0:T(8,128)(2,1)}), bf16[48,49,384]{2,1,0:T(8,128)(2,1)S(1)}, u32[]{:S(2)}, u32[]{:S(2)}) async-start(bf16[48,49,384]{2,1,0:T(8,128)(2,1)} %copy.138), calls=%async_computation | async-start | bytes 4128768 | tf_op jit(solution)/shard_map/all_to_all | solution.py:161
  15.6 40.0 %copy-start.21 = (f32[384]{0:T(512)}, f32[384]{0:T(512)S(1)}, u32[]{:S(2)}) copy-start(f32[384]{0:T(512)S(1)} %get-tuple-element.99) | copy-start | bytes 4612
  15.6 28.0 %copy-start.27 = (f32[384]{0:T(512)}, f32[384]{0:T(512)S(1)}, u32[]{:S(2)}) copy-start(f32[384]{0:T(512)S(1)} %get-tuple-element.183) | copy-start | bytes 4612
  15.6 28.0 %copy-start.30 = (f32[384]{0:T(512)}, f32[384]{0:T(512)S(1)}, u32[]{:S(2)}) copy-start(f32[384]{0:T(512)S(1)} %get-tuple-element.103) | copy-start | bytes 4612
  15.6 136.5 %copy-start.32 = (f32[384]{0:T(512)}, f32[384]{0:T(512)S(1)}, u32[]{:S(2)}) copy-start(f32[384]{0:T(512)S(1)} %get-tuple-element.102) | copy-start | bytes 4612
  15.7 39.9 %copy-start.34 = (f32[1,196]{1,0:T(1,128)}, f32[1,196]{1,0:T(1,128)S(1)}, u32[]{:S(2)}) copy-start(f32[1,196]{1,0:T(1,128)S(1)} %get-tuple-element.169) | copy-start | bytes 2356
  15.7 146.3 %copy-start.36 = (f32[1,196]{1,0:T(1,128)}, f32[1,196]{1,0:T(1,128)S(1)}, u32[]{:S(2)}) copy-start(f32[1,196]{1,0:T(1,128)S(1)} %get-tuple-element.168) | copy-start | bytes 2356
  16.0 39.6 %copy-start.18 = (bf16[1,196,196]{2,0,1:T(2,128)(2,1)}, bf16[1,196,196]{2,0,1:T(2,128)(2,1)S(1)}, u32[]{:S(2)}) copy-start(bf16[1,196,196]{2,0,1:T(2,128)(2,1)S(1)} %get-tuple-element.167) | copy-start | bytes 230500
  50.4 5.2 copy-start.14
  60.2 5.5 copy-start.47
  60.2 5.5 copy-start.48
  60.2 5.5 copy-start.49
  60.2 5.5 copy-start.50
  60.2 6.1 copy-start.29
  62.0 32.6 %all-to-all-start.1 = ((bf16[12,196,384]{2,0,1:T(8,128)(2,1)}), bf16[12,196,384]{2,0,1:T(8,128)(2,1)S(1)}, u32[]{:S(2)}, u32[]{:S(2)}) async-start(bf16[12,196,384]{2,0,1:T(8,128)(2,1)} %copy.142), calls=%async_computation.1 | async-start | bytes 4816896 | tf_op jit(solution)/shard_map/all_to_all | solution.py:174
  65.7 36.0 %copy-start.23 = (f32[384]{0:T(512)}, f32[384]{0:T(512)S(1)}, u32[]{:S(2)}) copy-start(f32[384]{0:T(512)S(1)} %get-tuple-element.185) | copy-start | bytes 4612
  65.7 36.0 %copy-start.25 = (f32[384]{0:T(512)}, f32[384]{0:T(512)S(1)}, u32[]{:S(2)}) copy-start(f32[384]{0:T(512)S(1)} %get-tuple-element.93) | copy-start | bytes 4612
  66.4 41.1 %copy-start.55 = (f32[384]{0:T(512)}, f32[384]{0:T(512)S(1)}, u32[]{:S(2)}) copy-start(f32[384]{0:T(512)S(1)} %get-tuple-element.97) | copy-start | bytes 4612
  66.4 246.4 %copy-start.38 = (f32[384]{0:T(512)}, f32[384]{0:T(512)S(1)}, u32[]{:S(2)}) copy-start(f32[384]{0:T(512)S(1)} %get-tuple-element.188) | copy-start | bytes 4612
  66.4 156.1 %copy-start.41 = (f32[1536]{0:T(1024)}, f32[1536]{0:T(1024)S(1)}, u32[]{:S(2)}) copy-start(f32[1536]{0:T(1024)S(1)} %get-tuple-element.88) | copy-start | bytes 18436
  156.8 5.2 copy-start.13
  166.6 5.4 copy-start.61
  168.4 32.6 %all-to-all-start.3 = ((bf16[12,196,384]{2,0,1:T(8,128)(2,1)}), bf16[12,196,384]{2,0,1:T(8,128)(2,1)S(1)}, u32[]{:S(2)}, u32[]{:S(2)}) async-start(bf16[12,196,384]{2,0,1:T(8,128)(2,1)} %copy.149), calls=%async_computation.3 | async-start | bytes 4816896 | tf_op jit(solution)/shard_map/all_to_all | solution.py:174
  172.1 5.7 copy-start.58
  210.9 6.6 copy-start.9
  222.5 11.0 %copy-start.17 = (bf16[2352,384]{1,0:T(8,128)(2,1)S(1)}, bf16[2352,384]{1,0:T(8,128)(2,1)}, u32[]{:S(2)}) copy-start(bf16[2352,384]{1,0:T(8,128)(2,1)} %convert_element_type.603) | copy-start | bytes 5419012
  222.5 11.0 %copy-start.60 = (bf16[2,1536,384]{2,1,0:T(8,128)(2,1)S(1)}, bf16[2,1536,384]{2,1,0:T(8,128)(2,1)}, u32[]{:S(2)}) copy-start(bf16[2,1536,384]{2,1,0:T(8,128)(2,1)} %param.28) | copy-start | bytes 7077892
  233.6 16.9 %copy-start.5 = (f32[2352,384]{1,0:T(8,128)S(1)}, f32[2352,384]{1,0:T(8,128)}, u32[]{:S(2)}) copy-start(f32[2352,384]{1,0:T(8,128)} %reshape.304) | copy-start | bytes 10838020
  233.6 16.9 %copy-start.16 = (f32[2352,384]{1,0:T(8,128)S(1)}, f32[2352,384]{1,0:T(8,128)}, u32[]{:S(2)}) copy-start(f32[2352,384]{1,0:T(8,128)} %reshape.299) | copy-start | bytes 10838020
  250.4 7.4 copy-start.7
  259.9 28.9 %all-to-all-start.4 = ((bf16[48,49,384]{2,1,0:T(8,128)(2,1)}), bf16[48,49,384]{2,1,0:T(8,128)(2,1)S(1)}, u32[]{:S(2)}, u32[]{:S(2)}) async-start(bf16[48,49,384]{2,1,0:T(8,128)(2,1)} %convert_element_type.607), calls=%async_computation.4 | async-start | bytes 4128768 | tf_op jit(solution)/shard_map/all_to_all | solution.py:190
  263.5 9.0 %copy-start.57 = (u32[32]{0:T(128)S(1)}, u32[32]{0:T(128)}, u32[]{:S(2)}) copy-start(u32[32]{0:T(128)} %constant.23) | copy-start | bytes 388
  263.5 285.2 %reduce-scatter.11.cloned.1.call-start = ((), (), s32[]{:S(2)}) async-start(), calls=%async_computation.13 | async-start | bytes 2949120 | tf_op jit(solution)/shard_map/reduce_scatter | solution.py:108
  297.5 5.2 copy-start.12
  309.1 32.6 %all-to-all-start.5 = ((bf16[12,196,384]{2,0,1:T(8,128)(2,1)}), bf16[12,196,384]{2,0,1:T(8,128)(2,1)S(1)}, u32[]{:S(2)}, u32[]{:S(2)}) async-start(bf16[12,196,384]{2,0,1:T(8,128)(2,1)} %copy.158), calls=%async_computation.5 | async-start | bytes 4816896 | tf_op jit(solution)/shard_map/all_to_all | solution.py:200
  312.7 236.1 %reduce-scatter.15.cloned.1.call-start = ((), (), s32[]{:S(2)}) async-start(), calls=%async_computation.15 | async-start | bytes 2949120 | tf_op jit(solution)/shard_map/reduce_scatter | solution.py:110
  323.8 225.0 %reduce-scatter.9.cloned.1.call-start = ((), (), s32[]{:S(2)}) async-start(), calls=%async_computation.12 | async-start | bytes 2949120 | tf_op jit(solution)/shard_map/reduce_scatter | solution.py:108
  354.0 19.1 %copy-start.4 = (f32[2352,384]{1,0:T(8,128)S(1)}, f32[2352,384]{1,0:T(8,128)}, u32[]{:S(2)}) copy-start(f32[2352,384]{1,0:T(8,128)} %reshape.303) | copy-start | bytes 10838020
  354.0 19.1 %copy-start.24 = (f32[384]{0:T(512)S(1)}, f32[384]{0:T(512)}, u32[]{:S(2)}) copy-start(f32[384]{0:T(512)} %copy-done.23) | copy-start | bytes 4612
  354.0 19.1 %copy-start.26 = (f32[384]{0:T(512)S(1)}, f32[384]{0:T(512)}, u32[]{:S(2)}) copy-start(f32[384]{0:T(512)} %copy-done.25) | copy-start | bytes 4612
  377.9 170.9 %reduce-scatter.13.cloned.1.call-start = ((), (), s32[]{:S(2)}) async-start(), calls=%async_computation.14 | async-start | bytes 2949120 | tf_op jit(solution)/shard_map/reduce_scatter | solution.py:110
  390.2 5.3 copy-start.8
  390.2 5.3 copy-start.37
  427.8 6.0 copy-start.56
  430.1 41.6 %all-to-all-start.6 = ((bf16[48,49,384]{2,1,0:T(8,128)(2,1)}), bf16[48,49,384]{2,1,0:T(8,128)(2,1)S(1)}, u32[]{:S(2)}, u32[]{:S(2)}) async-start(bf16[48,49,384]{2,1,0:T(8,128)(2,1)} %convert_element_type.626), calls=%async_computation.6 | async-start | bytes 4128768 | tf_op jit(solution)/shard_map/all_to_all | solution.py:190
  433.7 38.0 %copy-start.22 = (f32[384]{0:T(512)S(1)}, f32[384]{0:T(512)}, u32[]{:S(2)}) copy-start(f32[384]{0:T(512)} %copy-done.21) | copy-start | bytes 4612
  433.7 183.7 %all-reduce.29.cloned.1.call-start = ((), (), s32[]{:S(2)}) async-start(), calls=%async_computation.16 | async-start | bytes 253952 | tf_op jit(solution)/shard_map/psum | solution.py:81
  480.3 5.1 copy-start.31
  485.4 18.6 %copy-start.15 = (bf16[12,196,384]{2,1,0:T(8,128)(2,1)S(1)}, bf16[12,196,384]{2,1,0:T(8,128)(2,1)}, u32[]{:S(2)}) copy-start(bf16[12,196,384]{2,1,0:T(8,128)(2,1)} %convert_element_type.634) | copy-start | bytes 5419012
  485.4 18.6 %copy-start.19 = (bf16[1,196,196]{2,0,1:T(2,128)(2,1)S(1)}, bf16[1,196,196]{2,0,1:T(2,128)(2,1)}, u32[]{:S(2)}) copy-start(bf16[1,196,196]{2,0,1:T(2,128)(2,1)} %copy-done.18) | copy-start | bytes 230500
  485.4 18.6 %copy-start.35 = (f32[1,196]{1,0:T(1,128)S(1)}, f32[1,196]{1,0:T(1,128)}, u32[]{:S(2)}) copy-start(f32[1,196]{1,0:T(1,128)} %copy-done.34) | copy-start | bytes 2356
  498.7 38.2 %collective-permute-start = (f32[21,196]{1,0:T(8,128)S(1)}, f32[21,196]{1,0:T(8,128)S(1)}, u32[]{:S(2)}, u32[]{:S(2)}) collective-permute-start(f32[21,196]{1,0:T(8,128)S(1)} %slice.120), channel_id=1, source_target_pairs={{0,1},{1,2},{2,3},{4,5},{5,6},{6,7},{8,9},{9,10},{10,11},{12,13},{... | collective-permute-start | bytes 49400
  500.0 37.0 %collective-permute-start.1 = (f32[21,196]{1,0:T(8,128)S(1)}, f32[21,196]{1,0:T(8,128)S(1)}, u32[]{:S(2)}, u32[]{:S(2)}) collective-permute-start(f32[21,196]{1,0:T(8,128)S(1)} %slice.121), channel_id=1, source_target_pairs={{0,1},{1,2},{2,3},{4,5},{5,6},{6,7},{8,9},{9,10},{10,11},{12,13},{... | collective-permute-start | bytes 49400
  543.5 5.8 copy-start.10
  543.5 5.8 copy-start.39
  543.5 5.8 copy-start.42
  543.5 5.8 copy-start.59
  543.5 87.2 %all-to-all-start.7 = ((f32[12,196,384]{2,0,1:T(8,128)}), f32[12,196,384]{2,0,1:T(8,128)}, u32[]{:S(2)}, u32[]{:S(2)}) async-start(f32[12,196,384]{2,0,1:T(8,128)} %copy.166), calls=%async_computation.7 | async-start | bytes 9633792 | tf_op jit(solution)/shard_map/all_to_all | solution.py:200
  548.7 182.7 %all-reduce.31.cloned.1.call-start = ((), (), s32[]{:S(2)}) async-start(), calls=%async_computation.17 | async-start | bytes 4718592 | tf_op jit(solution)/shard_map/psum | solution.py:81
  (13 other events, 39.9 us)
Sparse Core Ops, SparseCore 0:
  272.6 35.5 reduce-scatter.10
  323.9 35.7 reduce-scatter.14
  378.0 34.9 reduce-scatter.8
  418.3 47.6 reduce-scatter.12
Sparse Core Ops, SparseCore 1:
  538.6 78.8 all-reduce.28
  621.8 109.6 all-reduce.30
where the time goes:
time: 754 us; the launch traced here: 744 us
  waiting for transfers between devices  251 us (33%)
  matrix products  186 us (25%)
  local copies, waits for them, and re-layouts  153 us (20%)
  other arithmetic  53.7 us (7%)
  blocking collectives  49.2 us (7%)
  starting transfers between devices  33 us (4%)
  between operations  19.1 us (3%)
    psum x2, waiting for transfers between devices, reduce_grads(): lax.psum((members[0], members[1], members[2], members[3], members[4], mem...  144 us
    all_to_all x2, waiting for transfers between devices, local(): lax.all_to_all(mixed_out, 'mix', split_axis=1, concat_axis=0, tiled=True)  42.6 us
    all_to_all x2, waiting for transfers between devices, local(): lax.all_to_all(row_grad.astype(jnp.bfloat16), 'mix', split_axis=0, concat...  37.6 us
    dot_general x2, matrix products, mlp_backward(): jnp.einsum('tc,hc->th', branch_grad, down_matrix, preferred_element_type=...  33 us
    dot_general x2, matrix products, mlp_apply(): jnp.einsum('gph,hc->gpc', active, down_matrix, preferred_element_type=jnp...  31.2 us
    unnamed x153, local copies, waits for them, and re-layouts  30.9 us
    all_to_all x1, blocking collectives, local(): lax.all_to_all(stream.astype(jnp.bfloat16), 'mix', split_axis=0, concat_a...  29.4 us
    all_to_all x1, waiting for transfers between devices, local(): lax.all_to_all(stream.astype(jnp.bfloat16), 'mix', split_axis=0, concat_a...  24.9 us
  transfers between devices with their start and end apart: 15, of which 8 were waited for; matrix products, arithmetic and copies ran while one was open for 35% of the time, Pallas kernels for 0%

commit v1 on v0

--- a/solution.py
+++ b/solution.py
@@ -78,39 +78,13 @@
 
 def reduce_grads(mix_part, mlp_part):
     members = tuple(mix_part) + tuple(mlp_part)
-    summed = lax.psum(
-        (
-            members[0],
-            members[1],
-            members[2],
-            members[3],
-            members[4],
-            members[5],
-            members[6],
-            members[7],
-            members[8],
-            members[9],
-            members[10],
-            members[11],
-        ),
-        "dp",
-    )
-    return tuple(
-        (
-            lax.psum_scatter(summed[0], "mix", scatter_dimension=0, tiled=True),
-            lax.psum_scatter(summed[1], "mix", scatter_dimension=0, tiled=True),
-            lax.psum_scatter(summed[2], "mix", scatter_dimension=0, tiled=True),
-            lax.psum_scatter(summed[3], "mix", scatter_dimension=0, tiled=True),
-            lax.psum_scatter(summed[4], "mix", scatter_dimension=0, tiled=True),
-            lax.psum_scatter(summed[5], "mix", scatter_dimension=0, tiled=True),
-            lax.psum_scatter(summed[6], "mix", scatter_dimension=0, tiled=True),
-            lax.psum_scatter(summed[7], "mix", scatter_dimension=0, tiled=True),
-            lax.psum_scatter(summed[8], "mix", scatter_dimension=1, tiled=True),
-            lax.psum_scatter(summed[9], "mix", scatter_dimension=0, tiled=True),
-            lax.psum_scatter(summed[10], "mix", scatter_dimension=0, tiled=True),
-            lax.psum_scatter(summed[11], "mix", scatter_dimension=0, tiled=True),
-        )
-    )
+    scattered = tuple(
+        lax.psum_scatter(
+            member, "mix", scatter_dimension=1 if place == 8 else 0, tiled=True
+        )
+        for place, member in enumerate(members)
+    )
+    return lax.psum(scattered, "dp")
 
 
 def local(
@@ -154,31 +128,33 @@
             down_bias[layer_index].astype(jnp.float32),
         )
 
-    stream = images_in.astype(jnp.float32)
+    whole = lax.all_to_all(images_in, "mix", split_axis=0, concat_axis=1, tiled=True)
+    whole_grad = lax.all_to_all(out_grad, "mix", split_axis=0, concat_axis=1, tiled=True)
+    own = whole.shape[0]
+    slot_weight = lax.dynamic_slice_in_dim(
+        slot_mask.astype(jnp.float32), lax.axis_index("mix") * own, own, 0
+    )[:, None, None]
+    stream = whole.astype(jnp.float32)
     image_inputs = []
     kept_rows = []
     for layer_index in range(layer_count):
-        whole = lax.all_to_all(
-            stream.astype(jnp.bfloat16), "mix", split_axis=0, concat_axis=1, tiled=True
-        )
-        image_inputs.append(whole)
-        image_stream = whole.astype(jnp.float32)
+        image_inputs.append(stream.astype(jnp.bfloat16))
         gain_terms = first_terms(layer_index)
         mixed_in, across = mix_across(
-            image_stream,
+            stream,
             gain_terms,
             mix_weight[layer_index],
             mix_bias[layer_index].astype(jnp.float32),
         )
-        mixed_out = (image_stream + gain_terms[2] * across).astype(jnp.bfloat16)
-        first_rows = lax.all_to_all(mixed_out, "mix", split_axis=1, concat_axis=0, tiled=True)
+        first_rows = (stream + gain_terms[2] * across).astype(jnp.bfloat16)
         kept_rows.append(first_rows)
         stream = mlp_apply(first_rows, second_terms(layer_index), mlp_terms(layer_index)).astype(
             jnp.float32
         )
-    slot_weight = slot_mask.astype(jnp.float32)[:, None, None]
-    output = (slot_weight * stream).astype(jnp.bfloat16)
-    carried = slot_weight * out_grad.astype(jnp.float32)
+    output = lax.all_to_all(
+        (slot_weight * stream).astype(jnp.bfloat16), "mix", split_axis=1, concat_axis=0, tiled=True
+    )
+    carried = slot_weight * whole_grad.astype(jnp.float32)
     per_layer = [None] * layer_count
     for layer_index in reversed(range(layer_count)):
         row_grad, mlp_part = mlp_backward(
@@ -187,18 +163,17 @@
             second_terms(layer_index),
             mlp_terms(layer_index),
         )
-        first_grad = lax.all_to_all(
-            row_grad.astype(jnp.bfloat16), "mix", split_axis=0, concat_axis=1, tiled=True
-        ).astype(jnp.float32)
-        image_carried, mix_part = mix_backward(
+        carried, mix_part = mix_backward(
             image_inputs[layer_index].astype(jnp.float32),
-            first_grad,
+            row_grad.astype(jnp.bfloat16).astype(jnp.float32),
             first_terms(layer_index),
             mix_weight[layer_index],
             mix_bias[layer_index].astype(jnp.float32),
         )
-        carried = lax.all_to_all(image_carried, "mix", split_axis=1, concat_axis=0, tiled=True)
         per_layer[layer_index] = reduce_grads(mix_part, mlp_part)
+    carried = lax.all_to_all(
+        carried.astype(jnp.bfloat16), "mix", split_axis=1, concat_axis=0, tiled=True
+    ).astype(jnp.float32)
     stacked = tuple(
         (
             jnp.stack([per_layer[level_index][member] for level_index in range(layer_count)])

time: 754 us -> 588 us (0.78)
  waiting for transfers between devices: 251 us -> 192 us
  local copies, waits for them, and re-layouts: 153 us -> 114 us
  blocking collectives: 49.2 us -> 21.5 us
  other arithmetic: 53.7 us -> 31.8 us
  starting transfers between devices: 33 us -> 22.2 us
  matrix products: 186 us -> 176 us
    all_to_all x7 -> x4, waiting for transfers between devices: 106 us -> 32.9 us  [the longest x1 21.5 us: local(): lax.all_to_all(images_in, 'mix', split_axis=0, concat_axis=1, tiled=True)]
    all_to_all x1 -> x0, blocking collectives: 29.4 us -> none  [local(): lax.all_to_all(stream.astype(jnp.bfloat16), 'mix', split_axis=0, concat_a...]
    psum x2, waiting for transfers between devices: 144 us -> 159 us  [reduce_grads(): return lax.psum(scattered, 'dp')]
    convert_element_type x15 -> x10, local copies, waits for them, and re-layouts: 54.2 us -> 39.4 us  [the longest x2 9.83 us: local(): row_grad.astype(jnp.bfloat16).astype(jnp.float32)]
    convert_element_type x4 -> x1, local copies, waits for them, and re-layouts: 17.3 us -> 4.82 us  [mlp_backward(): upstream = incoming.reshape(-1, channels).astype(jnp.float32)]
    unnamed x153 -> x114, local copies, waits for them, and re-layouts: 30.9 us -> 19 us
    another operation x2 -> x20, local copies, waits for them, and re-layouts: 1.32 us -> 12.1 us  [local(): jnp.stack([per_layer[level_index][member] for level_index in range(layer_...]
    all_to_all x7 -> x4, starting transfers between devices: 27.5 us -> 17 us  [the longest x1 4.53 us: local(): lax.all_to_all((slot_weight * stream).astype(jnp.bfloat16), 'mix', split_...]
  transfers between devices with their start and end apart: 15 -> 12, of which waited for: 8 -> 4; matrix products, arithmetic and copies ran while one was open for 35% -> 38% of each run, Pallas kernels for 0% -> 0%
where the time goes in v1:
time: 588 us; the launch traced here: 577 us
  waiting for transfers between devices  192 us (33%)
  matrix products  176 us (30%)
  local copies, waits for them, and re-layouts  114 us (19%)
  other arithmetic  31.8 us (5%)
  starting transfers between devices  22.2 us (4%)
  blocking collectives  21.5 us (4%)
  between operations  19.2 us (3%)
    psum x2, waiting for transfers between devices, reduce_grads(): return lax.psum(scattered, 'dp')  159 us
    dot_general x2, matrix products, mlp_backward(): jnp.einsum('tc,hc->th', branch_grad, down_matrix, preferred_element_type=...  31.5 us
    dot_general x2, matrix products, mlp_apply(): jnp.einsum('gph,hc->gpc', active, down_matrix, preferred_element_type=jnp...  26.9 us
    all_to_all x1, waiting for transfers between devices, local(): lax.all_to_all(images_in, 'mix', split_axis=0, concat_axis=1, tiled=True)  21.5 us
    unnamed x2, blocking collectives  21.5 us
    unnamed x114, local copies, waits for them, and re-layouts  19 us
    dot_general x2, matrix products, mlp_backward(): jnp.dot(normed, up_matrix, preferred_element_type=jnp.float32) + up_offset  18.7 us
    dot_general x2, matrix products, mix_backward(): jnp.einsum('pq,gpc->gqc', mix_matrix, across_grad, preferred_element_type...  17.5 us
  transfers between devices with their start and end apart: 12, of which 4 were waited for; matrix products, arithmetic and copies ran while one was open for 38% of the time, Pallas kernels for 0%

profile of v1, /device:TPU:0, one launch (start us, length us, event | category | flops | bytes accessed | tf_op | source)
XLA Modules:
  0.0 576.8 jit_solution(8548429631942026486)
XLA Ops:
  8.0 3.2 copy.92
  11.3 4.4 all-to-all-start
  15.9 3.3 copy.100
  19.4 21.5 %all-to-all-done = bf16[48,49,384]{2,1,0:T(8,128)(2,1)S(1)} async-done(((bf16[48,49,384]{2,1,0:T(8,128)(2,1)}), bf16[48,49,384]{2,1,0:T(8,128)(2,1)S(1)}, u32[]{:S(2)}, u32[]{:S(2)}) %all-to-all-start) | async-done | bytes 1806368 | tf_op jit(solution)/shard_map/all_to_all | solution.py:131
  41.0 4.5 all-to-all-start.2
  48.0 3.8 convert_element_type.489
  52.1 2.3 copy.93
  54.4 5.0 reshape.255
  59.5 11.4 %all-to-all-done.2 = bf16[48,49,384]{2,1,0:T(8,128)(2,1)} async-done(((bf16[48,49,384]{2,1,0:T(8,128)(2,1)}), bf16[48,49,384]{2,1,0:T(8,128)(2,1)}, u32[]{:S(2)}, u32[]{:S(2)}) %all-to-all-start.2) | async-done | bytes 1806368 | tf_op jit(solution)/shard_map/all_to_all | solution.py:132
  70.9 3.8 convert_bitcast_fusion
  74.6 3.1 convert_reduce_fusion.2
  77.9 2.1 convert_element_type.545
  80.0 4.5 copy.101
  84.5 5.2 reshape.274
  89.7 6.7 %add_convert_fusion.4 = (bf16[12,196,384]{2,1,0:T(8,128)(2,1)}, f32[12,196,384]{2,1,0:T(8,128)}, f32[12,384,196]{1,2,0:T(8,128)}) fusion(f32[384]{0:T(512)S(1)} %get-tuple-element.93, f32[384]{0:T(512)S(1)} %get-tuple-element.196, f32[12,196,384]{2,1,0:T(8,128)} %reshape.255, f32[196]{0:T(256)S(1)} %bitcast.203, f32[384]{0:T(512)S(1)} %get-tuple-element.99, ...), kind=kOutput, calls=%fused_computation.89 | convolution fusion | flops 361267200 | bytes 14532912 | tf_op jit(solution)/shard_map/pq,gqc->gpc/dot_general | solution.py:9
  96.4 12.9 %add_convert_fusion.3 = bf16[12,196,384]{2,1,0:T(8,128)(2,1)S(1)} fusion(f32[12,196,384]{2,1,0:T(8,128)} %get-tuple-element.165, f32[384]{0:T(512)S(1)} %get-tuple-element.97, f32[384]{0:T(512)S(1)} %get-tuple-element.95, bf16[12,196,384]{2,1,0:T(8,128)(2,1)} %get-tuple-element.164, f32[1536]{0:T(1024)S(1)} %get-tuple-element.89, ...), kind=kOutput, calls=%fused_computation.88 | convolution fusion | flops 5588803584 | bytes 9704448 | tf_op jit(solution)/shard_map/gph,hc->gpc/dot_general | solution.py:23
  109.3 4.8 add_convert_fusion.2
  114.1 3.6 convert_element_type.546
  117.8 4.8 reshape.280
  122.5 12.8 %multiply_convert_fusion = (bf16[2352,1536]{1,0:T(8,128)(2,1)}, f32[2352,1536]{1,0:T(8,128)}) fusion(f32[1536]{0:T(1024)S(1)} %get-tuple-element.88, bf16[2352,384]{1,0:T(8,128)(2,1)} %convert_element_type.546, bf16[2,384,1536]{2,1,0:T(8,128)(2,1)} %param.26), kind=kOutput, calls=%fused_computation.38 | convolution fusion | flops 2810658816 | bytes 24668160 | tf_op jit(solution)/shard_map/dot_general | solution.py:36
  135.3 15.3 %convert_reduce_fusion = (f32[1536]{0:T(1024)}, bf16[2352,1536]{1,0:T(8,128)(2,1)S(1)}) fusion(f32[2352,1536]{1,0:T(8,128)} %get-tuple-element.189, bf16[2352,384]{1,0:T(8,128)(2,1)S(1)} %copy-done.11, bf16[2,1536,384]{2,1,0:T(8,128)(2,1)} %param.28), kind=kOutput, calls=%fused_computation.36 | convolution fusion | flops 2854009344 | bytes 24668160 | tf_op jit(solution)/shard_map/tc,hc->th/dot_general | solution.py:44
  150.6 7.9 %fusion.128 = (f32[384]{0:T(512)}, f32[384]{0:T(512)}, f32[2352]{0:T(1024)S(1)}, bf16[2352,384]{1,0:T(8,128)(2,1)}, f32[2352,384]{1,0:T(8,128)}, /*index=5*/bf16[2352,384]{1,0:T(8,128)(2,1)S(1)}) fusion(f32[2352,384]{1,0:T(8,128)S(1)} %copy-done.3, f32[384]{0:T(512)S(1)} %get-tuple-element.197, f32[2352,384]{1,0:T(8,128)S(1)} %copy-done.7, ...), kind=kOutput, calls=%fused_computation.222 | convolution fusion | flops 2787173120 | bytes 22884544 | tf_op jit(solution)/shard_map/th,ch->tc/dot_general | solution.py:50
  159.8 8.0 %fusion.68 = f32[1536,384]{1,0:T(8,128)} fusion(bf16[2352,1536]{1,0:T(8,128)(2,1)} %get-tuple-element.188, bf16[2352,384]{1,0:T(8,128)(2,1)S(1)} %get-tuple-element.177, f32[384]{0:T(512)S(1)} %get-tuple-element.94), kind=kOutput, calls=%fused_computation.121 | convolution fusion | flops 2777241600 | bytes 11392512 | tf_op jit(solution)/shard_map/th,tc->hc/dot_general | solution.py:43
  171.6 9.3 %fusion.66 = f32[384,1536]{1,0:T(8,128)} fusion(bf16[2352,1536]{1,0:T(8,128)(2,1)} %copy-done.4, f32[2352,384]{1,0:T(8,128)} %reshape.280, f32[384]{0:T(512)S(1)} %get-tuple-element.92, f32[384]{0:T(512)S(1)} %get-tuple-element.197), kind=kOutput, calls=%fused_computation.119 | convolution fusion | flops 2777241600 | bytes 13200384 | tf_op jit(solution)/shard_map/tc,th->ch/dot_general | solution.py:49
  180.9 14.0 %multiply_convert_fusion.6 = bf16[12,196,384]{2,1,0:T(8,128)(2,1)} fusion(f32[12,196,384]{2,1,0:T(8,128)} %get-tuple-element.163, f32[384]{0:T(512)S(1)} %get-tuple-element.96, f32[384]{0:T(512)S(1)} %get-tuple-element.94, f32[12]{0:T(128)S(1)} %dynamic_slice.3, bf16[12,196,384]{2,1,0:T(8,128)(2,1)} %get-tuple-element.162, f32[1536]{0:T(1024)S(1)} %get-tuple-element.88, ...), kind=kOutput, calls=%fused_computation.85 | convolution fusion | flops 5591513088 | bytes 9704496 | tf_op jit(solution)/shard_map/gph,hc->gpc/dot_general | solution.py:23
  194.9 3.6 convert_element_type.560
  198.5 4.8 reshape.279
  203.3 3.3 copy.97
  206.6 4.5 all-to-all-start.1
  211.4 3.8 convert_element_type.553
  215.2 4.8 reshape.275
  220.0 9.4 %convert_reduce_fusion.3 = (f32[384]{0:T(512)S(1)}, bf16[12,196,384]{2,1,0:T(8,128)(2,1)}, f32[12,196,384]{2,1,0:T(8,128)}, f32[384]{0:T(512)S(1)}, f32[384]{0:T(512)S(1)}, /*index=5*/f32[12,384,196]{1,2,0:T(8,128)}) fusion(f32[384]{0:T(512)S(1)} %get-tuple-element.95, f32[12,196,384]{2,1,0:T(8,128)} %reshape.275, f32[384]{0:T(512)S(1)} %get-tuple-element.195, ...), kind=kOutput, calls=%fused_computation.80 | convolution fusion | flops 366685056 | bytes 19954992 | tf_op jit(solution)/shard_map/pq,gpc->gqc/dot_general | solution.py:70
  229.5 3.6 convert_element_type.559
  233.1 4.8 reshape.276
  237.9 5.9 %convolution_add_fusion = f32[2352,1536]{1,0:T(8,128)S(1)} fusion(bf16[2352,384]{1,0:T(8,128)(2,1)} %convert_element_type.560, f32[1536]{0:T(1024)S(1)} %get-tuple-element.89, bf16[2,384,1536]{2,1,0:T(8,128)(2,1)} %param.26), kind=kOutput, calls=%fused_computation.40 | convolution fusion | flops 2778144768 | bytes 17442816 | tf_op jit(solution)/shard_map/dot_general | solution.py:36
  243.9 5.1 copy-done.50
  249.0 6.8 %fusion.67 = f32[1536,384]{1,0:T(8,128)} fusion(f32[2352,384]{1,0:T(8,128)S(1)} %copy-done.8, f32[384]{0:T(512)S(1)} %get-tuple-element.95, f32[2352,1536]{1,0:T(8,128)S(1)} %convolution_add_fusion), kind=kOutput, calls=%fused_computation.120 | convolution fusion | flops 2808852480 | bytes 20424192 | tf_op jit(solution)/shard_map/th,tc->hc/dot_general | solution.py:43
  256.1 16.2 %convert_reduce_fusion.1 = (f32[1536]{0:T(1024)S(1)}, bf16[2352,1536]{1,0:T(8,128)(2,1)S(1)}) fusion(f32[2352,1536]{1,0:T(8,128)} %copy-done.50, bf16[2352,384]{1,0:T(8,128)(2,1)} %convert_element_type.559, bf16[2,1536,384]{2,1,0:T(8,128)(2,1)} %param.28), kind=kOutput, calls=%fused_computation.37 | convolution fusion | flops 2854009344 | bytes 24668160 | tf_op jit(solution)/shard_map/tc,hc->th/dot_general | solution.py:44
  272.4 7.3 %fusion.127 = (f32[384]{0:T(512)S(1)}, f32[384]{0:T(512)S(1)}, f32[2352]{0:T(1024)S(1)}, bf16[2352,384]{1,0:T(8,128)(2,1)}, f32[2352,384]{1,0:T(8,128)}) fusion(f32[2352,384]{1,0:T(8,128)S(1)} %copy-done.1, f32[2352,384]{1,0:T(8,128)S(1)} %copy-done.9, f32[384]{0:T(512)S(1)} %copy-done.18, f32[384]{0:T(512)S(1)} %copy-done.23, ...), kind=kOutput, calls=%fused_computation.221 | convolution fusion | flops 2784463616 | bytes 21065920 | tf_op jit(solution)/shard_map/th,ch->tc/dot_general | solution.py:50
  279.7 3.6 convert_element_type.567
  283.3 5.0 reshape.277
  288.4 3.0 fusion.98
  291.5 3.0 fusion.101
  294.7 7.8 %fusion.65 = f32[384,1536]{1,0:T(8,128)} fusion(bf16[2352,1536]{1,0:T(8,128)(2,1)} %copy-done.5, f32[2352,384]{1,0:T(8,128)S(1)} %copy-done.2, f32[384]{0:T(512)S(1)} %copy-done.16, f32[384]{0:T(512)S(1)} %copy-done.18), kind=kOutput, calls=%fused_computation.118 | convolution fusion | flops 2777241600 | bytes 13200384 | tf_op jit(solution)/shard_map/tc,th->ch/dot_general | solution.py:49
  302.6 8.0 %fusion.48 = (f32[384]{0:T(512)S(1)}, bf16[12,196,384]{2,1,0:T(8,128)(2,1)S(1)}, f32[384]{0:T(512)S(1)}, f32[12,384,196]{1,2,0:T(8,128)}) fusion(f32[12,196,384]{2,1,0:T(8,128)} %reshape.277, f32[12,384,196]{1,2,0:T(8,128)} %get-tuple-element.184, f32[196]{0:T(256)S(1)} %bitcast.204, f32[384]{0:T(512)S(1)} %copy-done.20, f32[12,196,384]{2,1,0:T(8,128)} %reshape.255, ...), kind=kOutput, calls=%fused_computation.79 | convolution fusion | flops 361266432 | bytes 18145584 | tf_op jit(solution)/shard_map/pq,gpc->gqc/dot_general | solution.py:70
  310.6 10.8 %fusion.129 = (f32[56,196]{1,0:T(8,128)S(1)}, f32[56,196]{1,0:T(8,128)S(1)}) fusion(f32[196,196]{1,0:T(8,128)S(1)} %fusion.98, f32[196,196]{1,0:T(8,128)S(1)} %fusion.101), kind=kCustom, calls=%all-reduce-scatter.2 | all-reduce-scatter fusion | flops 87809 | bytes 395648
  321.5 2.8 reduce_sum.179
  324.4 2.4 reduce_sum.178
  326.9 1.6 collective-permute-start
  328.5 2.6 collective-permute-start.1
  331.0 7.9 %fusion.78 = f32[384]{0:T(512)S(1)} fusion(f32[384]{0:T(512)S(1)} %get-tuple-element.96, bf16[2352,1536]{1,0:T(8,128)(2,1)} %get-tuple-element.188, bf16[2352,384]{1,0:T(8,128)(2,1)} %copy-done.49, bf16[2,1536,384]{2,1,0:T(8,128)(2,1)} %param.28), kind=kOutput, calls=%fused_computation.130 | convolution fusion | flops 2778144256 | bytes 10214400 | tf_op jit(solution)/shard_map/dot_general | solution.py:39
  339.0 8.9 %fusion.77 = f32[384]{0:T(512)S(1)} fusion(f32[2352,384]{1,0:T(8,128)S(1)} %copy-done.10, f32[384]{0:T(512)S(1)} %copy-done.41, bf16[2,1536,384]{2,1,0:T(8,128)(2,1)S(1)} %copy-done.47, f32[2352,1536]{1,0:T(8,128)} %copy-done.50), kind=kOutput, calls=%fused_computation.129 | convolution fusion | flops 2809755136 | bytes 19246592 | tf_op jit(solution)/shard_map/dot_general | solution.py:39
  348.0 10.7 %all-reduce.24 = (f32[384]{0:T(512)S(1)}, f32[384]{0:T(512)S(1)}, f32[384]{0:T(512)S(1)}, f32[384]{0:T(512)S(1)}, f32[384]{0:T(512)S(1)}, /*index=5*/f32[384]{0:...) all-reduce(f32[384]{0:T(512)S(1)} %get-tuple-element.170, ...), channel_id=3, replica_groups=mesh['dp'=8,'mix'=4] {'mix'}, use_global_device_ids=true, to_apply=%region_4.0.clone | all-reduce | flops 8840 | bytes 70720
  371.9 1.8 copy.105
  373.6 3.6 all-to-all-start.3
  377.3 73.3 %all-reduce.29.cloned.1.call-done = (f32[1,96]{1,0:T(1,128)}, f32[1,96]{1,0:T(1,128)}, f32[1,96]{1,0:T(1,128)}, f32[1,96]{1,0:T(1,128)}, f32[1,96]{1,0:T(1,128)}...) async-done(((f32[1,96]{1,0:T(1,128)}, f32[1,96]{1,0:T(1,128)}, ...) | async-done | bytes 85688 | tf_op jit(solution)/shard_map/psum | solution.py:87
  463.2 2.1 copy.99
  466.8 2.2 copy_convert_fusion
  469.0 4.9 reshape.285
  473.9 2.5 copy.107
  476.4 2.5 copy.109
  478.9 85.6 %all-reduce.31.cloned.1.call-done = (f32[1,384,384]{2,1,0:T(8,128)}, f32[1,384,384]{2,1,0:T(8,128)}, f32[1,384,384]{2,1,0:T(8,128)}, f32[1,384,384]{2,1,0:T(8,128)}) async-done(((f32[1,384,384]{2,1,0:T(8,128)}, f32[1,384,384]{2,1,0:T(8,128)}, f32[1,384,384]{2,1,0:T(8,128)}, f32[1,384,384]{2,1,0:T(8,128)}), (f32[1,384,384]{2,1,0:T(8,128)}, f32[1,384,384]{2,1,0:T(8,128)}, f32[1,384,384]{2,1,0:T(8,128)}, ...) | async-done | bytes 2359312 | tf_op jit(solution)/shard_map/psum | solution.py:87
  564.5 2.3 pad_maximum_fusion
  566.8 2.3 pad_maximum_fusion.1
  (180 shorter events, 34.0 us)
Async XLA Ops:
  8.0 7.6 %copy-start.48 = (s32[48]{0:T(128)S(1)}, s32[48]{0:T(128)}, u32[]{:S(2)}) copy-start(s32[48]{0:T(128)} %param.17) | copy-start | bytes 580
  11.2 8.0 %copy-start.32 = (bf16[2,384]{1,0:T(2,128)(2,1)S(1)}, bf16[2,384]{1,0:T(2,128)(2,1)}, u32[]{:S(2)}) copy-start(bf16[2,384]{1,0:T(2,128)(2,1)} %param.20) | copy-start | bytes 4612
  11.2 8.0 %copy-start.33 = (bf16[2,384]{1,0:T(2,128)(2,1)S(1)}, bf16[2,384]{1,0:T(2,128)(2,1)}, u32[]{:S(2)}) copy-start(bf16[2,384]{1,0:T(2,128)(2,1)} %param.25) | copy-start | bytes 4612
  11.3 8.0 %copy-start.34 = (bf16[2,384]{1,0:T(2,128)(2,1)S(1)}, bf16[2,384]{1,0:T(2,128)(2,1)}, u32[]{:S(2)}) copy-start(bf16[2,384]{1,0:T(2,128)(2,1)} %param.19) | copy-start | bytes 4612
  11.3 8.0 %copy-start.35 = (bf16[2,384]{1,0:T(2,128)(2,1)S(1)}, bf16[2,384]{1,0:T(2,128)(2,1)}, u32[]{:S(2)}) copy-start(bf16[2,384]{1,0:T(2,128)(2,1)} %param.18) | copy-start | bytes 4612
  11.3 8.1 %copy-start.36 = (bf16[2,384]{1,0:T(2,128)(2,1)S(1)}, bf16[2,384]{1,0:T(2,128)(2,1)}, u32[]{:S(2)}) copy-start(bf16[2,384]{1,0:T(2,128)(2,1)} %param.24) | copy-start | bytes 4612
  11.3 8.1 %copy-start.37 = (bf16[2,384]{1,0:T(2,128)(2,1)S(1)}, bf16[2,384]{1,0:T(2,128)(2,1)}, u32[]{:S(2)}) copy-start(bf16[2,384]{1,0:T(2,128)(2,1)} %param.23) | copy-start | bytes 4612
  11.3 29.7 %all-to-all-start = ((bf16[48,49,384]{2,1,0:T(8,128)(2,1)}), bf16[48,49,384]{2,1,0:T(8,128)(2,1)S(1)}, u32[]{:S(2)}, u32[]{:S(2)}) async-start(bf16[48,49,384]{2,1,0:T(8,128)(2,1)} %copy.92), calls=%async_computation | async-start | bytes 4128768 | tf_op jit(solution)/shard_map/all_to_all | solution.py:131
  15.9 29.6 %copy-start.38 = (bf16[2,384]{1,0:T(2,128)(2,1)S(1)}, bf16[2,384]{1,0:T(2,128)(2,1)}, u32[]{:S(2)}) copy-start(bf16[2,384]{1,0:T(2,128)(2,1)} %param.29) | copy-start | bytes 4612
  15.9 29.6 %copy-start.21 = (bf16[2,1536]{1,0:T(2,128)(2,1)S(1)}, bf16[2,1536]{1,0:T(2,128)(2,1)}, u32[]{:S(2)}) copy-start(bf16[2,1536]{1,0:T(2,128)(2,1)} %param.27) | copy-start | bytes 18436
  15.9 29.7 %copy-start.39 = (bf16[2,196]{1,0:T(2,128)(2,1)S(1)}, bf16[2,196]{1,0:T(2,128)(2,1)}, u32[]{:S(2)}) copy-start(bf16[2,196]{1,0:T(2,128)(2,1)} %param.22) | copy-start | bytes 2356
  15.9 29.7 %copy-start.14 = (bf16[2,196,196]{2,0,1:T(2,128)(2,1)S(1)}, bf16[2,196,196]{2,0,1:T(2,128)(2,1)}, u32[]{:S(2)}) copy-start(bf16[2,196,196]{2,0,1:T(2,128)(2,1)} %param.21) | copy-start | bytes 460996
  19.2 70.4 %copy-start.22 = (f32[384]{0:T(512)}, f32[384]{0:T(512)S(1)}, u32[]{:S(2)}) copy-start(f32[384]{0:T(512)S(1)} %get-tuple-element.99) | copy-start | bytes 4612
  19.4 27.1 %copy-start.19 = (f32[384]{0:T(512)}, f32[384]{0:T(512)S(1)}, u32[]{:S(2)}) copy-start(f32[384]{0:T(512)S(1)} %get-tuple-element.194) | copy-start | bytes 4612
  19.4 27.1 %copy-start.24 = (f32[384]{0:T(512)}, f32[384]{0:T(512)S(1)}, u32[]{:S(2)}) copy-start(f32[384]{0:T(512)S(1)} %get-tuple-element.103) | copy-start | bytes 4612
  19.4 89.9 %copy-start.26 = (f32[384]{0:T(512)}, f32[384]{0:T(512)S(1)}, u32[]{:S(2)}) copy-start(f32[384]{0:T(512)S(1)} %get-tuple-element.102) | copy-start | bytes 4612
  19.4 70.3 %copy-start.15 = (f32[384]{0:T(512)}, f32[384]{0:T(512)S(1)}, u32[]{:S(2)}) copy-start(f32[384]{0:T(512)S(1)} %get-tuple-element.93) | copy-start | bytes 4612
  19.4 70.2 %copy-start.17 = (f32[384]{0:T(512)}, f32[384]{0:T(512)S(1)}, u32[]{:S(2)}) copy-start(f32[384]{0:T(512)S(1)} %get-tuple-element.196) | copy-start | bytes 4612
  41.0 29.9 %all-to-all-start.2 = ((bf16[48,49,384]{2,1,0:T(8,128)(2,1)}), bf16[48,49,384]{2,1,0:T(8,128)(2,1)}, u32[]{:S(2)}, u32[]{:S(2)}) async-start(bf16[48,49,384]{2,1,0:T(8,128)(2,1)} %copy.100), calls=%async_computation.2 | async-start | bytes 4128768 | tf_op jit(solution)/shard_map/all_to_all | solution.py:132
  45.4 325.9 %reduce-scatter.15.cloned.1.call-start = ((), (), s32[]{:S(2)}) async-start(), calls=%async_computation.11 | async-start | bytes 2949120 | tf_op jit(solution)/shard_map/reduce_scatter | solution.py:82
  45.5 50.8 %copy-start.40 = (f32[384]{0:T(512)}, f32[384]{0:T(512)S(1)}, u32[]{:S(2)}) copy-start(f32[384]{0:T(512)S(1)} %get-tuple-element.97) | copy-start | bytes 4612
  45.6 44.0 %copy-start.28 = (f32[1,196]{1,0:T(1,128)}, f32[1,196]{1,0:T(1,128)S(1)}, u32[]{:S(2)}) copy-start(f32[1,196]{1,0:T(1,128)S(1)} %get-tuple-element.181) | copy-start | bytes 2356
  45.9 43.8 %copy-start.12 = (bf16[1,196,196]{2,0,1:T(2,128)(2,1)}, bf16[1,196,196]{2,0,1:T(2,128)(2,1)S(1)}, u32[]{:S(2)}) copy-start(bf16[1,196,196]{2,0,1:T(2,128)(2,1)S(1)} %get-tuple-element.179) | copy-start | bytes 230500
  84.5 5.2 copy-start.6
  122.5 12.8 %copy-start.11 = (bf16[2352,384]{1,0:T(8,128)(2,1)S(1)}, bf16[2352,384]{1,0:T(8,128)(2,1)}, u32[]{:S(2)}) copy-start(bf16[2352,384]{1,0:T(8,128)(2,1)} %convert_element_type.545) | copy-start | bytes 5419012
  135.3 15.3 %copy-start.3 = (f32[2352,384]{1,0:T(8,128)S(1)}, f32[2352,384]{1,0:T(8,128)}, u32[]{:S(2)}) copy-start(f32[2352,384]{1,0:T(8,128)} %reshape.280) | copy-start | bytes 10838020
  135.3 15.3 %copy-start.7 = (f32[2352,384]{1,0:T(8,128)S(1)}, f32[2352,384]{1,0:T(8,128)}, u32[]{:S(2)}) copy-start(f32[2352,384]{1,0:T(8,128)} %reshape.274) | copy-start | bytes 10838020
  135.3 15.3 %copy-start.45 = (bf16[2,384,1536]{2,1,0:T(8,128)(2,1)S(1)}, bf16[2,384,1536]{2,1,0:T(8,128)(2,1)}, u32[]{:S(2)}) copy-start(bf16[2,384,1536]{2,1,0:T(8,128)(2,1)} %param.26) | copy-start | bytes 7077892
  150.6 8.0 %copy-start.4 = (bf16[2352,1536]{1,0:T(8,128)(2,1)}, bf16[2352,1536]{1,0:T(8,128)(2,1)S(1)}, u32[]{:S(2)}) copy-start(bf16[2352,1536]{1,0:T(8,128)(2,1)S(1)} %get-tuple-element.191) | copy-start | bytes 21676036
  158.6 1.3 copy-start.49
  159.8 8.5 %copy-start.44 = (u32[32]{0:T(128)S(1)}, u32[32]{0:T(128)}, u32[]{:S(2)}) copy-start(u32[32]{0:T(128)} %constant.33) | copy-start | bytes 388
  167.9 203.5 %reduce-scatter.11.cloned.1.call-start = ((), (), s32[]{:S(2)}) async-start(), calls=%async_computation.9 | async-start | bytes 2949120 | tf_op jit(solution)/shard_map/reduce_scatter | solution.py:82
  206.6 167.0 %all-to-all-start.1 = ((bf16[12,196,384]{2,0,1:T(8,128)(2,1)}), bf16[12,196,384]{2,0,1:T(8,128)(2,1)}, u32[]{:S(2)}, u32[]{:S(2)}) async-start(bf16[12,196,384]{2,0,1:T(8,128)(2,1)} %copy.97), calls=%async_computation.1 | async-start | bytes 4816896 | tf_op jit(solution)/shard_map/all_to_all | solution.py:154
  211.2 160.2 %reduce-scatter.13.cloned.1.call-start = ((), (), s32[]{:S(2)}) async-start(), calls=%async_computation.10 | async-start | bytes 2949120 | tf_op jit(solution)/shard_map/reduce_scatter | solution.py:82
  237.9 11.1 %copy-start.8 = (f32[2352,384]{1,0:T(8,128)S(1)}, f32[2352,384]{1,0:T(8,128)}, u32[]{:S(2)}) copy-start(f32[2352,384]{1,0:T(8,128)} %reshape.276) | copy-start | bytes 10838020
  243.8 5.1 copy-start.50
  255.8 16.5 %copy-start.18 = (f32[384]{0:T(512)S(1)}, f32[384]{0:T(512)}, u32[]{:S(2)}) copy-start(f32[384]{0:T(512)} %copy-done.17) | copy-start | bytes 4612
  255.8 16.5 %copy-start.23 = (f32[384]{0:T(512)S(1)}, f32[384]{0:T(512)}, u32[]{:S(2)}) copy-start(f32[384]{0:T(512)} %copy-done.22) | copy-start | bytes 4612
  255.8 115.6 %reduce-scatter.9.cloned.1.call-start = ((), (), s32[]{:S(2)}) async-start(), calls=%async_computation.8 | async-start | bytes 2949120 | tf_op jit(solution)/shard_map/reduce_scatter | solution.py:82
  256.1 16.3 %copy-start.1 = (f32[2352,384]{1,0:T(8,128)S(1)}, f32[2352,384]{1,0:T(8,128)}, u32[]{:S(2)}) copy-start(f32[2352,384]{1,0:T(8,128)} %reshape.279) | copy-start | bytes 10838020
  256.1 16.3 %copy-start.9 = (f32[2352,384]{1,0:T(8,128)S(1)}, f32[2352,384]{1,0:T(8,128)}, u32[]{:S(2)}) copy-start(f32[2352,384]{1,0:T(8,128)} %reshape.276) | copy-start | bytes 10838020
  256.1 16.3 %copy-start.46 = (bf16[2,384,1536]{2,1,0:T(8,128)(2,1)S(1)}, bf16[2,384,1536]{2,1,0:T(8,128)(2,1)}, u32[]{:S(2)}) copy-start(bf16[2,384,1536]{2,1,0:T(8,128)(2,1)} %param.26) | copy-start | bytes 7077892
  272.3 7.3 %copy-start.5 = (bf16[2352,1536]{1,0:T(8,128)(2,1)}, bf16[2352,1536]{1,0:T(8,128)(2,1)S(1)}, u32[]{:S(2)}) copy-start(bf16[2352,1536]{1,0:T(8,128)(2,1)S(1)} %get-tuple-element.193) | copy-start | bytes 21676036
  283.3 5.0 copy-start.27
  288.3 3.2 copy-start
  288.3 3.2 copy-start.20
  288.4 3.2 copy-start.25
  291.5 3.1 copy-start.2
  291.5 3.1 copy-start.16
  294.6 7.9 %copy-start.13 = (bf16[1,196,196]{2,0,1:T(2,128)(2,1)S(1)}, bf16[1,196,196]{2,0,1:T(2,128)(2,1)}, u32[]{:S(2)}) copy-start(bf16[1,196,196]{2,0,1:T(2,128)(2,1)} %copy-done.12) | copy-start | bytes 230500
  294.7 7.9 %copy-start.29 = (f32[1,196]{1,0:T(1,128)S(1)}, f32[1,196]{1,0:T(1,128)}, u32[]{:S(2)}) copy-start(f32[1,196]{1,0:T(1,128)} %copy-done.28) | copy-start | bytes 2356
  302.5 148.1 %all-reduce.29.cloned.1.call-start = ((), (), s32[]{:S(2)}) async-start(), calls=%async_computation.12 | async-start | bytes 251904 | tf_op jit(solution)/shard_map/psum | solution.py:87
  326.9 12.1 %copy-start.10 = (f32[2352,384]{1,0:T(8,128)S(1)}, f32[2352,384]{1,0:T(8,128)}, u32[]{:S(2)}) copy-start(f32[2352,384]{1,0:T(8,128)} %reshape.276) | copy-start | bytes 10838020
  326.9 12.1 %copy-start.41 = (f32[384]{0:T(512)S(1)}, f32[384]{0:T(512)}, u32[]{:S(2)}) copy-start(f32[384]{0:T(512)} %copy-done.40) | copy-start | bytes 4612
  326.9 12.1 %copy-start.47 = (bf16[2,1536,384]{2,1,0:T(8,128)(2,1)S(1)}, bf16[2,1536,384]{2,1,0:T(8,128)(2,1)}, u32[]{:S(2)}) copy-start(bf16[2,1536,384]{2,1,0:T(8,128)(2,1)} %param.28) | copy-start | bytes 7077892
  326.9 42.8 %collective-permute-start = (f32[21,196]{1,0:T(8,128)S(1)}, f32[21,196]{1,0:T(8,128)S(1)}, u32[]{:S(2)}, u32[]{:S(2)}) collective-permute-start(f32[21,196]{1,0:T(8,128)S(1)} %slice.120), channel_id=1, source_target_pairs={{0,1},{1,2},{2,3},{4,5},{5,6},{6,7},{8,9},{9,10},{10,11},{12,13},{... | collective-permute-start | bytes 49400
  328.5 41.3 %collective-permute-start.1 = (f32[21,196]{1,0:T(8,128)S(1)}, f32[21,196]{1,0:T(8,128)S(1)}, u32[]{:S(2)}, u32[]{:S(2)}) collective-permute-start(f32[21,196]{1,0:T(8,128)S(1)} %slice.121), channel_id=1, source_target_pairs={{0,1},{1,2},{2,3},{4,5},{5,6},{6,7},{8,9},{9,10},{10,11},{12,13},{... | collective-permute-start | bytes 49400
  339.0 8.9 %copy-start.30 = (f32[384]{0:T(512)S(1)}, f32[384]{0:T(512)}, u32[]{:S(2)}) copy-start(f32[384]{0:T(512)} %get-tuple-element.153) | copy-start | bytes 4612
  339.0 8.9 %copy-start.31 = (f32[1536]{0:T(1024)S(1)}, f32[1536]{0:T(1024)}, u32[]{:S(2)}) copy-start(f32[1536]{0:T(1024)} %get-tuple-element.190) | copy-start | bytes 18436
  339.0 8.9 %copy-start.42 = (f32[384]{0:T(512)S(1)}, f32[384]{0:T(512)}, u32[]{:S(2)}) copy-start(f32[384]{0:T(512)} %get-tuple-element.86) | copy-start | bytes 4612
  339.0 8.9 %copy-start.43 = (f32[384]{0:T(512)S(1)}, f32[384]{0:T(512)}, u32[]{:S(2)}) copy-start(f32[384]{0:T(512)} %get-tuple-element.87) | copy-start | bytes 4612
  371.3 193.2 %all-reduce.31.cloned.1.call-start = ((), (), s32[]{:S(2)}) async-start(), calls=%async_computation.13 | async-start | bytes 4718592 | tf_op jit(solution)/shard_map/psum | solution.py:87
  373.6 93.1 %all-to-all-start.3 = ((bf16[12,196,384]{2,0,1:T(8,128)(2,1)}), bf16[12,196,384]{2,0,1:T(8,128)(2,1)S(1)}, u32[]{:S(2)}, u32[]{:S(2)}) async-start(bf16[12,196,384]{2,0,1:T(8,128)(2,1)} %copy.105), calls=%async_computation.3 | async-start | bytes 4816896 | tf_op jit(solution)/shard_map/all_to_all | solution.py:174
Sparse Core Ops, SparseCore 0:
  168.0 34.2 reduce-scatter.14
  204.8 45.8 reduce-scatter.10
  255.9 35.6 reduce-scatter.12
  302.6 35.7 reduce-scatter.8
Sparse Core Ops, SparseCore 1:
  371.4 79.2 all-reduce.28
  454.9 109.6 all-reduce.30

commit v2 on v1

v2 whole, which is shorter than its diff:
```python
import functools
import math

import jax
import jax.numpy as jnp
from jax import lax
from jax.experimental import pallas as pl
from jax.experimental.pallas import tpu as pltpu
from jax.sharding import PartitionSpec as P

MESH = pl.DeviceIdType.MESH
F32 = jnp.float32
BF16 = jnp.bfloat16
GROUP = 16
TILE = 16
TANH_A = math.sqrt(2.0 / math.pi)
TANH_B = TANH_A * 0.044715


def dot(a, b):
    return jnp.dot(a, b, preferred_element_type=F32)


def dot_nt(a, b):
    return lax.dot_general(a, b, (((1,), (1,)), ((), ())), preferred_element_type=F32)


def iota(shape, axis):
    return lax.broadcasted_iota(jnp.int32, shape, axis)


def gelu_pair(value):
    square = value * value
    curve = jnp.tanh(value * (TANH_A + TANH_B * square))
    half = 0.5 * value
    gate = 0.5 * curve + 0.5
    slope = gate + (half * (1.0 - curve * curve)) * (TANH_A + (3.0 * TANH_B) * square)
    return value * gate, slope


def mask_lanes(mask_ref, first, count, pick):
    total = jnp.zeros(pick.shape, F32)
    for k in range(count):
        total = jnp.where(pick == k, mask_ref[first + k].astype(F32), total)
    return total


def swap_matrix():
    side = GROUP * TILE
    row, lane = iota((side, side), 0), iota((side, side), 1)
    return jnp.where((row >> 4) + ((row & 15) << 4) == lane, 1.0, 0.0)


class Sizes:
    def __init__(self, parts, slots, patches, channels, hidden, layers):
        self.parts = parts
        self.slots = slots
        self.patches = patches
        self.channels = channels
        self.hidden = hidden
        self.layers = layers
        self.groups = slots // GROUP
        self.mine = GROUP // parts
        self.main = patches // TILE * TILE
        self.block = self.mine * self.main
        self.body = parts * self.block
        self.rows = self.body + parts * self.mine
        self.image = parts * self.main
        self.mix_rows = self.image + parts * self.mine
        self.ones = self.mix_rows
        self.mix_cols = self.mix_rows + TILE
        self.pad = -(-self.mix_cols // 128) * 128
        self.left = -(-self.groups * self.mine // TILE) * TILE
        self.whole = parts * patches


def whole_kernel(
    z,
    keep,
    x_hbm, dy_hbm, mask_ref, mixw_ref, mixb_ref,
    mgain_ref, mshift_ref, mscale_ref, pgain_ref, pshift_ref, pscale_ref, downb_ref, upb_ref,
    up_hbm, down_hbm,
    out_w, out_e, dx_w, dx_e, du_hbm, dd_hbm, dm_ref, dv_ref, dub_ref,
    du_ref, dd_ref, stage, send_x, send_dy, sende_x, sende_dy, got_x, got_dy,
    xs, firsts, dys, outs_left, out_left, act, slope, up_w, down_w, mix_m, mix_t,
    load_sem, own_sem, send_sem, recv_sem, lsend_sem, lrecv_sem,
):
    dp, me = lax.axis_index("dp"), lax.axis_index("mix")
    parts, groups, channels, hidden = z.parts, z.groups, z.channels, z.hidden
    peers = [lax.rem(me + r, parts) for r in range(parts)]

    loads = []
    for k, hbm in enumerate((x_hbm, dy_hbm)):
        for g in range(groups):
            loads.append(
                pltpu.make_async_copy(
                    hbm.at[:, pl.ds(g * GROUP, GROUP), :], stage.at[g], load_sem.at[k * groups + g]
                )
            )
    w_loads = [
        pltpu.make_async_copy(up_hbm, up_w, load_sem.at[2 * groups]),
        pltpu.make_async_copy(down_hbm, down_w, load_sem.at[2 * groups + 1]),
    ]
    for copy in loads[:groups] + w_loads:
        copy.start()

    barrier = pltpu.get_barrier_semaphore()
    for r in range(1, parts):
        pl.semaphore_signal(barrier, inc=1, device_id=(dp, peers[r]), device_id_type=MESH)

    swap = swap_matrix()
    swap_b = swap.astype(BF16)
    left_all = parts * z.left

    def convert(send, g, matrix):
        for t in range(z.main // TILE):
            block = stage[g, t * TILE : (t + 1) * TILE].reshape(TILE * GROUP, channels)
            rows = dot(matrix, block).astype(BF16).reshape(GROUP, TILE, channels)
            for d in range(parts):
                for j in range(z.mine):
                    send[g, d, j * z.main + t * TILE : j * z.main + (t + 1) * TILE, :] = rows[
                        d * z.mine + j
                    ]

    def convert_left(send, lanes):
        row, lane = iota((left_all, z.slots), 0), iota((left_all, z.slots), 1)
        want = jnp.full(row.shape, -1, jnp.int32)
        for d in range(parts):
            for g in range(groups):
                base = d * z.left + g * z.mine
                inside = (row >= base) & (row < base + z.mine)
                want = jnp.where(inside, row - base + g * GROUP + d * z.mine, want)
        matrix = jnp.where(want == lane, 1.0, 0.0)
        if lanes is not None:
            matrix = matrix * lanes
        last = jnp.concatenate([stage[g, z.patches - 1] for g in range(groups)], axis=0)
        send[...] = dot(matrix.astype(BF16), last).astype(BF16).reshape(parts, z.left, channels)

    def exchange(k, g, send, target):
        copies = [pltpu.make_async_copy(send.at[g, me], target.at[g, pl.ds(me * z.block, z.block)], own_sem.at[k, g])]
        for r in range(1, parts):
            copies.append(
                pltpu.make_async_remote_copy(
                    src_ref=send.at[g, peers[r]],
                    dst_ref=target.at[g, pl.ds(me * z.block, z.block)],
                    send_sem=send_sem.at[k, g, r],
                    recv_sem=recv_sem.at[k, g, r],
                    device_id=(dp, peers[r]),
                    device_id_type=MESH,
                )
            )
        return copies

    def part_of(source, g, d):
        if len(source.shape) == 4:
            return source.at[g, d]
        return source.at[g, pl.ds(d * z.block, z.block)]

    def exchange_back(k, g, source, target):
        copies = [pltpu.make_async_copy(part_of(source, g, me), target.at[g, me], own_sem.at[k, g])]
        for r in range(1, parts):
            copies.append(
                pltpu.make_async_remote_copy(
                    src_ref=part_of(source, g, peers[r]),
                    dst_ref=target.at[g, me],
                    send_sem=send_sem.at[k, g, r],
                    recv_sem=recv_sem.at[k, g, r],
                    device_id=(dp, peers[r]),
                    device_id_type=MESH,
                )
            )
        return copies

    def exchange_left(k, send, target):
        copies = [pltpu.make_async_copy(send.at[me], target.at[me], lsend_sem.at[k, 0])]
        for r in range(1, parts):
            copies.append(
                pltpu.make_async_remote_copy(
                    src_ref=send.at[peers[r]],
                    dst_ref=target.at[me],
                    send_sem=lsend_sem.at[k, r],
                    recv_sem=lrecv_sem.at[k, r],
                    device_id=(dp, peers[r]),
                    device_id_type=MESH,
                )
            )
        return copies

    def start(copies):
        for copy in copies:
            copy.start()

    def arrive(copies):
        copies[0].wait()
        for copy in copies[1:]:
            copy.wait_recv()

    def sent(copies):
        for copy in copies[1:]:
            copy.wait_send()

    for g in range(groups):
        loads[g].wait()
        convert(send_x, g, swap_b)
        if g == 0:
            pl.semaphore_wait(barrier, parts - 1)
        start(exchange(0, g, send_x, xs.at[0]))
    convert_left(sende_x, None)
    for copy in loads[groups:]:
        copy.start()
    start(exchange_left(0, sende_x, got_x))
    for g in range(groups):
        loads[groups + g].wait()
        pick = iota((1, GROUP * TILE), 1) & 15
        lanes = mask_lanes(mask_ref, g * GROUP, GROUP, pick)
        convert(send_dy, g, (swap * lanes).astype(BF16))
        start(exchange(1, g, send_dy, dys))
    convert_left(sende_dy, mask_lanes(mask_ref, 0, z.slots, iota((1, z.slots), 1)))
    start(exchange_left(1, sende_dy, got_dy))

    size = (z.pad, z.whole)
    row, lane = iota(size, 0), iota(size, 1)
    want = row
    for m in range(1, parts):
        want = want + jnp.where(row >= m * z.main, 1, 0)
    for m in range(parts):
        base = z.image + m * z.mine
        inside = (row >= base) & (row < base + z.mine)
        want = jnp.where(inside, m * z.patches + z.patches - 1, want)
    want = jnp.where(row < z.mix_rows, want, -1)
    pick = jnp.where(want == lane, 1.0, 0.0).astype(BF16)
    spot = jnp.where((iota((z.pad, TILE), 0) == z.ones) & (iota((z.pad, TILE), 1) == 0), 1.0, 0.0)
    for l in range(z.layers):
        half = dot(pick, mixw_ref[:, l, :]).astype(BF16)
        offset = jnp.where(iota((TILE, z.whole), 0) == 0, mixb_ref[l : l + 1, :].astype(F32), 0.0)
        column = dot_nt(pick, offset.astype(BF16)).astype(BF16)
        full = dot_nt(half, pick) + dot_nt(column, spot.astype(BF16))
        mix_m[l] = full.astype(BF16)
        mix_t[l] = full.T.astype(BF16)

    for ref in (dm_ref, dv_ref, dub_ref):
        ref[...] = jnp.zeros(ref.shape, F32)

    def spread_left(got, target):
        tile = parts * z.mine
        row, lane = iota((groups * tile, left_all), 0), iota((groups * tile, left_all), 1)
        want = jnp.full(row.shape, -1, jnp.int32)
        for g in range(groups):
            for m in range(parts):
                base = g * tile + m * z.mine
                inside = (row >= base) & (row < base + z.mine)
                want = jnp.where(inside, row - base + m * z.left + g * z.mine, want)
        matrix = jnp.where(want == lane, 1.0, 0.0).astype(BF16)
        rows = dot(matrix, got[...].reshape(left_all, channels)).astype(BF16)
        for g in range(groups):
            target[g, z.body :, :] = rows[g * tile : (g + 1) * tile]

    def gather_left(source, target):
        tile = parts * z.mine
        row, lane = iota((left_all, groups * tile), 0), iota((left_all, groups * tile), 1)
        want = jnp.full(row.shape, -1, jnp.int32)
        for g in range(groups):
            for m in range(parts):
                base = m * z.left + g * z.mine
                inside = (row >= base) & (row < base + z.mine)
                want = jnp.where(inside, row - base + g * tile + m * z.mine, want)
        matrix = jnp.where(want == lane, 1.0, 0.0).astype(BF16)
        low = 0 if source.shape[1] == tile else z.body
        rows = jnp.concatenate([source[g, low:, :] for g in range(groups)], axis=0)
        target[...] = dot(matrix, rows).astype(BF16).reshape(parts, z.left, channels)

    def vector(ref, l):
        return ref[l : l + 1, :].astype(F32)

    tile_rows = parts * z.mine
    image_of = iota((tile_rows, 1), 0) & (z.mine - 1)
    ones_tile = jnp.where(iota((TILE, channels), 0) == 0, 1.0, 0.0).astype(BF16)

    def image_rows(ref, l, g, j):
        index = (g,) if l is None else (l, g)
        return [
            ref[(*index, pl.ds(m * z.block + j * z.main, z.main), slice(None))] for m in range(parts)
        ]

    def mixed_rows(l, g, j, left):
        gain, shift = vector(mgain_ref, l), vector(mshift_ref, l)
        pieces = [
            (gain * part.astype(F32) + shift).astype(BF16) for part in image_rows(xs, l, g, j)
        ]
        pieces.append(jnp.where(image_of == j, gain * left + shift, 0.0).astype(BF16))
        pieces.append(ones_tile)
        return jnp.concatenate(pieces, axis=0)

    def mix_forward(l, g):
        scale = vector(mscale_ref, l)
        left = xs[l, g, z.body :, :].astype(F32)
        left_total = jnp.zeros((tile_rows, channels), F32)
        for j in range(z.mine):
            mixed = mixed_rows(l, g, j, left)
            across = dot(mix_m[l, : z.mix_rows, : z.mix_cols], mixed)
            for m, part in enumerate(image_rows(xs, l, g, j)):
                rows = part.astype(F32) + scale * across[m * z.main : (m + 1) * z.main]
                firsts[l, g, pl.ds(m * z.block + j * z.main, z.main), :] = rows.astype(BF16)
            left_total = jnp.where(image_of == j, across[z.image :], left_total)
        firsts[l, g, z.body :, :] = (left + scale * left_total).astype(BF16)

    chunk = 512 if hidden % 512 == 0 else 128

    def slot_of(l, g):
        return l * groups + g if keep else 0

    def mlp_hidden(l, g, normed, at):
        bias = upb_ref[l : l + 1, :].astype(F32)
        for h in range(0, hidden, chunk):
            value = dot(normed, up_w[l, :, h : h + chunk]) + bias[:, h : h + chunk]
            active, grade = gelu_pair(value)
            active = active.astype(BF16)
            act[at, :, h : h + chunk] = active
            slope[at, :, h : h + chunk] = grade.astype(BF16)
            yield h, active

    def mlp_normed(l, g):
        rows = firsts[l, g].astype(F32)
        return rows, (vector(pgain_ref, l) * rows + vector(pshift_ref, l)).astype(BF16)

    def mlp_forward(l, g, target):
        rows, normed = mlp_normed(l, g)
        total = None
        for h, active in mlp_hidden(l, g, normed, slot_of(l, g)):
            term = dot(active, down_w[l, h : h + chunk, :])
            total = term if total is None else total + term
        result = rows + vector(pscale_ref, l) * (total + vector(downb_ref, l))
        result = result.astype(BF16)
        if target is not None:
            target[g] = result
        else:
            sent(exchange(0, g, send_x, xs.at[0]))
            send_x[g] = result[: z.body].reshape(parts, z.block, channels)
            outs_left[g] = result[z.body :]

    def mlp_backward(l, g):
        rows, normed = mlp_normed(l, g)
        at = slot_of(l, g)
        if not keep:
            for _ in mlp_hidden(l, g, normed, at):
                pass
        upper = dys[g].astype(F32)
        branch = (vector(pscale_ref, l) * upper).astype(BF16)
        dv_ref[l, 5:6, :] += jnp.sum(branch.astype(F32), axis=0, keepdims=True)
        normed_t, branch_t = normed.T, branch.T
        total = None
        for h in range(0, hidden, chunk):
            span = slice(h, h + chunk)
            back = dot_nt(branch, down_w[l, span, :])
            grad = (back * slope[at, :, span].astype(F32)).astype(BF16)
            dub_ref[l, :, span] += jnp.sum(grad.astype(F32), axis=0, keepdims=True)
            du_ref[:, span] += dot(normed_t, grad)
            dd_ref[:, span] += dot(branch_t, act[at, :, span])
            term = dot_nt(grad, up_w[l, :, span])
            total = term if total is None else total + term
        dv_ref[l, 3:4, :] += jnp.sum(total * rows, axis=0, keepdims=True)
        dv_ref[l, 4:5, :] += jnp.sum(total, axis=0, keepdims=True)
        dys[g] = (upper + vector(pgain_ref, l) * total).astype(BF16)

    def mix_backward(l, g, target):
        gain, scale = vector(mgain_ref, l), vector(mscale_ref, l)
        left = xs[l, g, z.body :, :].astype(F32)
        left_grad = dys[g, z.body :, :].astype(F32)
        left_total = jnp.zeros((tile_rows, channels), F32)
        sums = [jnp.zeros((1, channels), F32) for _ in range(3)]
        for j in range(z.mine):
            mixed = mixed_rows(l, g, j, left)
            grads = [part.astype(F32) for part in image_rows(dys, None, g, j)]
            pieces = [(scale * part).astype(BF16) for part in grads]
            pieces.append(jnp.where(image_of == j, scale * left_grad, 0.0).astype(BF16))
            across = jnp.concatenate(pieces, axis=0)
            dm_ref[l, : z.mix_rows, : z.mix_cols] += dot_nt(across, mixed)
            back = dot(mix_t[l, : z.mix_cols, : z.mix_rows], across)
            for m, part in enumerate(image_rows(xs, l, g, j)):
                some = back[m * z.main : (m + 1) * z.main]
                sums[0] += jnp.sum(some * part.astype(F32), axis=0, keepdims=True)
                sums[1] += jnp.sum(some, axis=0, keepdims=True)
                target[g, pl.ds(m * z.block + j * z.main, z.main), :] = (
                    grads[m] + gain * some
                ).astype(BF16)
            left_total = jnp.where(image_of == j, back[z.image : z.mix_rows], left_total)
            sums[2] += back[z.ones : z.ones + 1]
        sums[0] += jnp.sum(left_total * left, axis=0, keepdims=True)
        sums[1] += jnp.sum(left_total, axis=0, keepdims=True)
        target[g, z.body :, :] = (left_grad + gain * left_total).astype(BF16)
        for k in range(3):
            dv_ref[l, k : k + 1, :] += sums[k]

    for copy in w_loads:
        copy.wait()
    arrive(exchange_left(0, sende_x, got_x))
    spread_left(got_x, xs.at[0])

    def forward(g, carry):
        arrive(exchange(0, g, send_x, xs.at[0]))
        for l in range(z.layers):
            mix_forward(l, g)
            mlp_forward(l, g, xs.at[l + 1] if l + 1 < z.layers else None)
        return carry

    lax.fori_loop(0, groups, forward, 0)
    gather_left(outs_left, out_left)

    arrive(exchange_left(1, sende_dy, got_dy))
    spread_left(got_dy, dys)

    def backward(l):
        def step(g, carry):
            if l == z.layers - 1:
                arrive(exchange(1, g, send_dy, dys))
                start(exchange_back(2, g, send_x, out_w))
            mlp_backward(l, g)
            mix_backward(l, g, dys)
            if l == 0:
                start(exchange_back(3, g, dys, dx_w))
            return carry

        return step

    for l in reversed(range(z.layers)):
        for ref in (du_ref, dd_ref):
            ref[...] = jnp.zeros(ref.shape, F32)
        lax.fori_loop(0, groups, backward(l), 0)
        if l == z.layers - 1:
            start(exchange_left(2, out_left, out_e))

        turned = dd_ref[...] * down_w[l].astype(F32).T
        dv_ref[l, 6:7, :] = jnp.sum(turned, axis=1)[None, :]
        dv_ref[l, 6:7, :] += vector(downb_ref, l) * dv_ref[l, 5:6, :]
        dv_ref[l, 6:7, :] = dv_ref[l, 6:7, :] / vector(pscale_ref, l)
        total = vector(mgain_ref, l) * dv_ref[l, 0:1, :] + vector(mshift_ref, l) * dv_ref[l, 1:2, :]
        dv_ref[l, 2:3, :] = (total + dv_ref[l, 2:3, :]) / vector(mscale_ref, l)
        keeps = [
            pltpu.make_async_copy(du_ref, du_hbm.at[l], load_sem.at[0]),
            pltpu.make_async_copy(dd_ref, dd_hbm.at[l], load_sem.at[1]),
        ]
        for copy in keeps:
            copy.start()
        for copy in keeps:
            copy.wait()

    for g in range(groups):
        sent(exchange(1, g, send_dy, dys))
    sent(exchange_left(0, sende_x, got_x))
    sent(exchange_left(1, sende_dy, got_dy))
    gather_left(dys, sende_x)
    last = exchange_left(3, sende_x, dx_e)
    start(last)
    for copies in [exchange_left(2, out_left, out_e), last]:
        arrive(copies)
        sent(copies)
    for g in range(groups):
        for copies in [exchange_back(2, g, send_x, out_w), exchange_back(3, g, dys, dx_w)]:
            arrive(copies)
            sent(copies)


def finish_kernel(z, mask_ref, out_w, out_e, dx_w, dx_e, out_ref, dx_ref):
    g = pl.program_id(0)
    swap = swap_matrix()
    pick = iota((1, GROUP * TILE), 1) >> 4
    masked = (swap * mask_lanes(mask_ref, g * GROUP, GROUP, pick)).astype(BF16)
    left_all = z.parts * z.left
    row, lane = iota((GROUP, left_all), 0), iota((GROUP, left_all), 1)
    want = row + g * z.mine
    for d in range(1, z.parts):
        want = want + jnp.where(row >= d * z.mine, z.left - z.mine, 0)
    last = jnp.where(want == lane, 1.0, 0.0)
    lanes = jnp.zeros((GROUP, 1), F32)
    for k in range(GROUP):
        lanes = jnp.where(iota((GROUP, 1), 0) == k, mask_ref[g * GROUP + k].astype(F32), lanes)
    for wire, left, target, matrix, tail in (
        (out_w, out_e, out_ref, masked, (last * lanes).astype(BF16)),
        (dx_w, dx_e, dx_ref, swap.astype(BF16), last.astype(BF16)),
    ):
        for t in range(z.main // TILE):
            block = jnp.concatenate(
                [
                    wire[0, i * z.main + t * TILE : i * z.main + (t + 1) * TILE, :]
                    for i in range(GROUP)
                ],
                axis=0,
            )
            rows = dot(matrix, block).reshape(TILE, GROUP, z.channels)
            target[t * TILE : (t + 1) * TILE] = rows.astype(target.dtype)
        rows = dot(tail, left[...].reshape(left_all, z.channels))
        target[z.patches - 1] = rows.astype(target.dtype)


def local(parts, images_in, out_grad, slot_mask, mix_gain, mix_shift, mix_scale, mix_weight, mix_bias,
          mlp_gain, mlp_shift, mlp_scale, up_weight, up_bias, down_weight, down_bias):
    slots, patches, channels = images_in.shape
    layers, _, hidden = up_weight.shape
    z = Sizes(parts, slots, patches, channels, hidden, layers)
    keep = layers * z.groups * z.rows * hidden * 4 <= 30e6
    kept = layers * z.groups if keep else 1
    vmem = pl.BlockSpec(memory_space=pltpu.VMEM)
    smem = pl.BlockSpec(memory_space=pltpu.SMEM)
    hbm = pl.BlockSpec(memory_space=pl.ANY)
    wire = jax.ShapeDtypeStruct((z.groups, parts, z.block, channels), BF16)
    left = jax.ShapeDtypeStruct((parts, z.left, channels), BF16)
    dma = pltpu.SemaphoreType.DMA
    rows = (z.groups, z.rows, channels)
    out_w, out_e, dx_w, dx_e, du, dd, dm, dv, dub = pl.pallas_call(
        functools.partial(whole_kernel, z, keep),
        out_shape=(
            wire, left, wire, left,
            jax.ShapeDtypeStruct((layers, channels, hidden), F32),
            jax.ShapeDtypeStruct((layers, channels, hidden), F32),
            jax.ShapeDtypeStruct((layers, z.pad, z.pad), F32),
            jax.ShapeDtypeStruct((layers, 8, channels), F32),
            jax.ShapeDtypeStruct((layers, 1, hidden), F32),
        ),
        in_specs=[hbm, hbm, smem] + [vmem] * 10 + [hbm, hbm],
        out_specs=(hbm,) * 6 + (vmem,) * 3,
        scratch_shapes=[
            pltpu.VMEM((channels, hidden), F32),
            pltpu.VMEM((channels, hidden), F32),
            pltpu.VMEM((z.groups, patches, GROUP, channels), BF16),
            pltpu.VMEM((z.groups, parts, z.block, channels), BF16),
            pltpu.VMEM((z.groups, parts, z.block, channels), BF16),
            pltpu.VMEM((parts, z.left, channels), BF16),
            pltpu.VMEM((parts, z.left, channels), BF16),
            pltpu.VMEM((parts, z.left, channels), BF16),
            pltpu.VMEM((parts, z.left, channels), BF16),
            pltpu.VMEM((layers, *rows), BF16),
            pltpu.VMEM((layers, *rows), BF16),
            pltpu.VMEM(rows, BF16),
            pltpu.VMEM((z.groups, parts * z.mine, channels), BF16),
            pltpu.VMEM((parts, z.left, channels), BF16),
            pltpu.VMEM((kept, z.rows, hidden), BF16),
            pltpu.VMEM((kept, z.rows, hidden), BF16),
            pltpu.VMEM((layers, channels, hidden), BF16),
            pltpu.VMEM((layers, hidden, channels), BF16),
            pltpu.VMEM((layers, z.pad, z.pad), BF16),
            pltpu.VMEM((layers, z.pad, z.pad), BF16),
            dma((2 * z.groups + 2,)),
            dma((4, z.groups)),
            dma((4, z.groups, parts)),
            dma((4, z.groups, parts)),
            dma((4, parts)),
            dma((4, parts)),
        ],
        compiler_params=pltpu.CompilerParams(
            collective_id=0, has_side_effects=True, vmem_limit_bytes=64 << 20
        ),
        name="layers",
    )(
        jnp.transpose(images_in, (1, 0, 2)),
        jnp.transpose(out_grad, (1, 0, 2)),
        slot_mask,
        jnp.transpose(mix_weight, (1, 0, 2)),
        mix_bias, mix_gain, mix_shift, mix_scale, mlp_gain, mlp_shift, mlp_scale, down_bias, up_bias,
        up_weight, down_weight,
    )

    flat = (z.groups, parts * z.block, channels)
    block = pl.BlockSpec((1, *flat[1:]), lambda g: (g, 0, 0))
    whole = pl.BlockSpec(left.shape, lambda g: (0, 0, 0))
    turned = pl.BlockSpec((patches, GROUP, channels), lambda g: (0, g, 0))
    output, input_grad = pl.pallas_call(
        functools.partial(finish_kernel, z),
        grid=(z.groups,),
        out_shape=(
            jax.ShapeDtypeStruct((patches, slots, channels), BF16),
            jax.ShapeDtypeStruct((patches, slots, channels), F32),
        ),
        in_specs=[smem, block, whole, block, whole],
        out_specs=(turned, turned),
        name="finish",
    )(slot_mask, out_w.reshape(flat), out_e, dx_w.reshape(flat), dx_e)
    output = jnp.transpose(output, (1, 0, 2))
    input_grad = jnp.transpose(input_grad, (1, 0, 2))

    main = dm[:, : z.image, : z.image].reshape(layers, parts, z.main, parts, z.main)
    edge_q = dm[:, : z.image, z.image : z.mix_rows].reshape(layers, parts, z.main, parts, z.mine).sum(-1)
    edge_p = dm[:, z.image : z.mix_rows, : z.image].reshape(layers, parts, z.mine, parts, z.main).sum(2)
    corner = dm[:, z.image : z.mix_rows, z.image : z.mix_rows].reshape(layers, parts, z.mine, parts, z.mine).sum((2, 4))
    top = jnp.concatenate([main, edge_q[..., None]], axis=-1)
    low = jnp.concatenate([edge_p, corner[..., None]], axis=-1)
    weight = jnp.concatenate([top, low[:, :, None]], axis=2).reshape(layers, z.whole, z.whole)
    bias_main = dm[:, : z.image, z.ones].reshape(layers, parts, z.main)
    bias_edge = dm[:, z.image : z.mix_rows, z.ones].reshape(layers, parts, z.mine).sum(-1)
    bias = jnp.concatenate([bias_main, bias_edge[..., None]], axis=-1).reshape(layers, z.whole)
    shares = [dv[:, 0], dv[:, 1], dv[:, 2], weight, bias, dv[:, 3], dv[:, 4], dv[:, 6], du, dub[:, 0], dd, dv[:, 5]]
    axes = [1, 1, 1, 1, 1, 1, 1, 1, 2, 1, 2, 1]
    shares = tuple(
        lax.psum_scatter(share, "mix", scatter_dimension=axis, tiled=True)
        for share, axis in zip(shares, axes)
    )
    grads = list(lax.psum(shares, "dp"))
    grads[10] = jnp.swapaxes(grads[10], 1, 2)
    return (output, input_grad, *grads)


def solution(mesh):
    in_specs = (P("dp", "mix", None), P("dp", "mix", None), P("dp")) + (P(),) * 12
    out_specs = (
        P("dp", "mix", None),
        P("dp", "mix", None),
        P(None, "mix"),
        P(None, "mix"),
        P(None, "mix"),
        P(None, "mix", None),
        P(None, "mix"),
        P(None, "mix"),
        P(None, "mix"),
        P(None, "mix"),
        P(None, None, "mix"),
        P(None, "mix"),
        P(None, "mix", None),
        P(None, "mix"),
    )
    return jax.shard_map(
        functools.partial(local, mesh.shape["mix"]),
        mesh=mesh,
        in_specs=in_specs,
        out_specs=out_specs,
        check_vma=False,
    )
```

time: 588 us -> 567 us (0.964); the launches traced: 577 us -> 566 us
  matrix products: 176 us -> 0 us
  waiting for transfers between devices: 192 us -> 365 us
  Pallas kernels: 0 us -> 111 us
  local copies, waits for them, and re-layouts: 114 us -> 29.3 us
  other arithmetic: 31.8 us -> 0.87 us
  blocking collectives: 21.5 us -> 44.8 us
  starting transfers between devices: 22.2 us -> 0.49 us
    unnamed x8 -> x21, waiting for transfers between devices: 0.52 us -> 187 us
    dot_general x20 -> x0, matrix products: 176 us -> none  [the longest x2 31.5 us: mlp_backward(): jnp.einsum('tc,hc->th', branch_grad, down_matrix, preferred_element_type=...]
    pallas_call x0 -> x2, Pallas kernels: none -> 111 us  [the longest x1 105 us: local(): pl.pallas_call(functools.partial(whole_kernel, z, keep), out_shape=(wire,...]
    reduce_scatter x4 -> x2, waiting for transfers between devices: 0.07 us -> 100 us  [local(): lax.psum_scatter(share, 'mix', scatter_dimension=axis, tiled=True)]
    psum x2 -> x1, waiting for transfers between devices: 159 us -> 77.9 us  [local(): grads = list(lax.psum(shares, 'dp'))]
    convert_element_type x21 -> x0, local copies, waits for them, and re-layouts: 78.3 us -> none  [the longest x2 9.83 us: local(): row_grad.astype(jnp.bfloat16).astype(jnp.float32)]
    psum x0 -> x1, blocking collectives: none -> 39 us  [local(): grads = list(lax.psum(shares, 'dp'))]
    all_to_all x4 -> x0, waiting for transfers between devices: 32.9 us -> none  [the longest x1 21.5 us: local(): lax.all_to_all(images_in, 'mix', split_axis=0, concat_axis=1, tiled=True)]
  transfers between devices with their start and end apart: 12 -> 12, of which waited for: 4 -> 12; matrix products, arithmetic and copies ran while one was open for 38% -> 3% of each run, Pallas kernels for 0% -> 1%
where the time goes in v2:
time: 567 us; the launch traced here: 566 us
  waiting for transfers between devices  365 us (64%)
  Pallas kernels  111 us (20%)
  blocking collectives  44.8 us (8%)
  local copies, waits for them, and re-layouts  29.3 us (5%)
  between operations  15 us (3%)
    unnamed x21, waiting for transfers between devices  187 us
    pallas_call x1, Pallas kernels, local(): pl.pallas_call(functools.partial(whole_kernel, z, keep), out_shape=(wire,...  105 us
    reduce_scatter x2, waiting for transfers between devices, local(): lax.psum_scatter(share, 'mix', scatter_dimension=axis, tiled=True)  100 us
    psum x1, waiting for transfers between devices, local(): grads = list(lax.psum(shares, 'dp'))  77.9 us
    psum x1, blocking collectives, local(): grads = list(lax.psum(shares, 'dp'))  39 us
    unnamed x32, local copies, waits for them, and re-layouts  20.6 us
  transfers between devices with their start and end apart: 12, of which 12 were waited for; matrix products, arithmetic and copies ran while one was open for 3% of the time, Pallas kernels for 1%

profile of v2, /device:TPU:0, one launch (start us, length us, event | category | flops | bytes accessed | tf_op | source)
XLA Modules:
  0.0 566.3 jit_solution(13436705609438302334)
XLA Ops:
  7.2 105.1 %layers.1 = (bf16[3,4,192,384]{3,2,1,0:T(8,128)(2,1)}, bf16[4,16,384]{2,1,0:T(8,128)(2,1)}, bf16[3,4,192,384]{3,2,1,0:T(8,128)(2,1)}, bf16[4,16,384]{2,1,0:T(8,1...) custom-call(bf16[49,48,384]{2,1,0:T(8,128)(2,1)} %bitcast.51, ...), custom_call_target="tpu_custom_call" | custom-call | tf_op jit(solution)/shard_map/layers/pallas_call | solution.py:509
  112.3 0.8 slice.45
  113.1 0.8 slice.44
  113.9 1.0 slice.43
  114.9 1.0 slice.42
  116.0 0.1 reshape.56
  116.1 0.1 reshape.57
  116.2 0.1 reduce_sum.38
  116.3 0.1 copy.42
  116.4 0.1 copy.39
  116.5 0.1 reshape.55
  116.7 0.4 reshape.54
  117.1 0.4 copy.41
  117.5 0.1 maximum_bitcast_fusion
  117.6 0.5 pad_maximum_fusion
  118.0 0.4 reshape.80
  118.4 1.0 copy.69
  119.5 0.7 reduce-scatter.28.cloned.1.call-update
  120.2 0.7 reduce-scatter.30.cloned.1.call-update
  121.0 0.8 copy.74
  121.9 0.8 copy.72
  122.8 0.8 copy.71
  123.7 0.8 copy.70
  124.6 0.8 copy.66
  125.5 0.8 copy.65
  126.4 0.8 copy.64
  127.3 1.2 copy.73
  128.6 0.6 dynamic-slice
  129.8 23.2 %all-reduce.7.cloned.1.call-done = f32[2,196,196]{2,0,1:T(2,128)} async-done(((f32[2,196,196]{2,0,1:T(2,128)}), f32[2,196,196]{2,0,1:T(2,128)}) %all-reduce.7.cloned.1.call-update) | async-done | bytes 307344
  153.0 1.5 constant_dynamic-slice_fusion.1
  154.5 49.6 %reduce-scatter.28.cloned.1.call-done = f32[2,384,384]{2,1,0:T(8,128)} async-done(((f32[2,384,1536]{2,1,0:T(8,128)}), f32[2,384,384]{2,1,0:T(8,128)}) %reduce-scatter.28.cloned.1.call-update) | async-done | bytes 1179664 | tf_op jit(solution)/shard_map/reduce_scatter | solution.py:593
  204.1 50.4 %reduce-scatter.30.cloned.1.call-done = f32[2,384,384]{2,1,0:T(8,128)} async-done(((f32[2,384,1536]{2,1,0:T(8,128)}), f32[2,384,384]{2,1,0:T(8,128)}) %reduce-scatter.30.cloned.1.call-update) | async-done | bytes 1179664 | tf_op jit(solution)/shard_map/reduce_scatter | solution.py:593
  254.6 1.2 slice_reduce_fusion
  255.8 0.1 reshape_squeeze.6
  255.8 0.9 slice_reduce_fusion.1
  256.7 0.1 reshape_squeeze.7
  256.8 0.1 reduce_sum.39
  256.9 0.1 copy.44
  257.0 0.1 pad_maximum_fusion.1
  257.1 0.1 reshape.59
  257.2 5.9 %finish.1 = (bf16[49,48,384]{2,1,0:T(8,128)(2,1)}, f32[49,48,384]{2,1,0:T(8,128)}) custom-call(s32[48]{0:T(128)} %mask_ref.3, bf16[3,768,384]{2,1,0:T(8,128)(2,1)} %bitcast.53, bf16[4,16,384]{2,1,0:T(8,128)(2,1)} %get-tuple-element.26.out_e, bf16[3,768,384]{2,1,0:T(8,128)(2,1)} %bitcast.54, bf16[4,16,384]{2,1,0:T(8,128)(2,1)} %get-tuple-element.28.dx_e), custom_call_target="tpu_custom_call" | custom-call | tf_op jit(solution)/shard_map/finish/pallas_call | solution.py:566
  263.0 5.7 %all-reduce.1 = f32[2,196]{1,0:T(2,128)S(1)} all-reduce(f32[2,196]{1,0:T(2,128)S(1)} %reshape.59), channel_id=6, replica_groups=mesh['dp'=8,'mix'=4] {'mix'}, use_global_device_ids=true, to_apply=%region_12.0.clone | all-reduce | flops 392 | bytes 3136
  268.8 0.1 constant_dynamic-slice_fusion
  268.8 7.9 %reduce-scatter.46.cloned.1.call-done = f32[96,2]{1,0:T(8,128)} async-done(((f32[384,2]{1,0:T(8,128)}), f32[96,2]{1,0:T(8,128)}) %reduce-scatter.46.cloned.1.call-update) | async-done | bytes 784
  276.8 0.9 copy.63
  277.6 21.3 %reduce-scatter.42.cloned.1.call-done = f32[96,2]{1,0:T(8,128)} async-done(((f32[384,2]{1,0:T(8,128)}), f32[96,2]{1,0:T(8,128)}) %reduce-scatter.42.cloned.1.call-update) | async-done | bytes 784
  299.0 0.9 copy.59
  299.8 21.3 %reduce-scatter.40.cloned.1.call-done = f32[96,2]{1,0:T(8,128)} async-done(((f32[384,2]{1,0:T(8,128)}), f32[96,2]{1,0:T(8,128)}) %reduce-scatter.40.cloned.1.call-update) | async-done | bytes 784
  321.2 0.9 copy.57
  322.0 21.5 %reduce-scatter.38.cloned.1.call-done = f32[96,2]{1,0:T(8,128)} async-done(((f32[384,2]{1,0:T(8,128)}), f32[96,2]{1,0:T(8,128)}) %reduce-scatter.38.cloned.1.call-update) | async-done | bytes 784
  343.5 0.9 copy.55
  344.4 21.5 %reduce-scatter.36.cloned.1.call-done = f32[96,2]{1,0:T(8,128)} async-done(((f32[384,2]{1,0:T(8,128)}), f32[96,2]{1,0:T(8,128)}) %reduce-scatter.36.cloned.1.call-update) | async-done | bytes 784
  365.9 0.9 copy.51
  366.7 21.5 %reduce-scatter.34.cloned.1.call-done = f32[96,2]{1,0:T(8,128)} async-done(((f32[384,2]{1,0:T(8,128)}), f32[96,2]{1,0:T(8,128)}) %reduce-scatter.34.cloned.1.call-update) | async-done | bytes 784
  388.2 0.9 copy.49
  389.1 21.4 %reduce-scatter.32.cloned.1.call-done = f32[96,2]{1,0:T(8,128)} async-done(((f32[384,2]{1,0:T(8,128)}), f32[96,2]{1,0:T(8,128)}) %reduce-scatter.32.cloned.1.call-update) | async-done | bytes 784
  410.5 0.9 copy.47
  411.3 25.7 %reduce-scatter.44.cloned.1.call-done = f32[384,2]{1,0:T(8,128)} async-done(((f32[1536,2]{1,0:T(8,128)}), f32[384,2]{1,0:T(8,128)}) %reduce-scatter.44.cloned.1.call-update) | async-done | bytes 3088
  437.0 1.0 copy.61
  438.1 39.0 %all-reduce.2 = (f32[2,96]{1,0:T(2,128)}, f32[2,96]{1,0:T(2,128)}, f32[2,96]{1,0:T(2,128)}, f32[2,49]{1,0:T(2,128)}, f32[2,96]{1,0:T(2,128)}, /*index=5*/f32[2,9...) all-reduce(f32[2,96]{1,0:T(2,128)S(1)} %copy.47, ...), channel_id=1, replica_groups=mesh['dp'=8,'mix'=4] {'dp'}, use_global_device_ids=true, to_apply=%region_1.0 | all-reduce | flops 2210 | bytes 17680 | tf_op jit(solution)/shard_map/psum | solution.py:596
  477.1 77.9 %all-reduce.9.cloned.1.call-done = (f32[2,49,196]{2,0,1:T(2,128)}, f32[2,384,384]{2,1,0:T(8,128)}, f32[2,384,384]{1,2,0:T(8,128)}) async-done(((f32[2,49,196]{2,0,1:T(2,128)}, f32[2,384,384]{2,1,0:T(8,128)}, f32[2,384,384]{1,2,0:T(8,128)}), (f32[2,49,196]{2,0,1:T(2,128)}, f32[2,384,384]{2,1,0:T(8,128)}, f32[2,384,384]{1,2,0:T(8,128)})) %all-reduce.9.cloned.1.call-update) | async-done | bytes 2436144 | tf_op jit(solution)/shard_map/psum | solution.py:596
  555.0 2.8 copy.45
  557.8 0.6 copy.79
  558.4 1.0 copy.80
  (35 shorter events, 0.7 us)
Async XLA Ops:
  7.2 145.8 %all-reduce.7.cloned.1.call-start = ((), (), s32[]{:S(2)}) async-start(), calls=%async_computation.20 | async-start | bytes 802816
  119.4 84.7 %reduce-scatter.28.cloned.1.call-start = ((), (), s32[]{:S(2)}) async-start(), calls=%async_computation.10 | async-start | bytes 5898240 | tf_op jit(solution)/shard_map/reduce_scatter | solution.py:593
  120.2 134.4 %reduce-scatter.30.cloned.1.call-start = ((), (), s32[]{:S(2)}) async-start(), calls=%async_computation.11 | async-start | bytes 5898240 | tf_op jit(solution)/shard_map/reduce_scatter | solution.py:593
  120.2 0.7 copy-start.2
  120.9 6.4 %copy-start.3 = (f32[2,1,1536]{2,1,0:T(1,128)S(1)}, f32[2,1,1536]{2,1,0:T(1,128)}, u32[]{:S(2)}) copy-start(f32[2,1,1536]{2,1,0:T(1,128)} %get-tuple-element.34) | copy-start | bytes 36868
  120.9 155.8 %reduce-scatter.46.cloned.1.call-start = ((), (), s32[]{:S(2)}) async-start(), calls=%async_computation.19 | async-start | bytes 245760
  121.8 177.1 %reduce-scatter.42.cloned.1.call-start = ((), (), s32[]{:S(2)}) async-start(), calls=%async_computation.17 | async-start | bytes 245760
  122.7 198.4 %reduce-scatter.40.cloned.1.call-start = ((), (), s32[]{:S(2)}) async-start(), calls=%async_computation.16 | async-start | bytes 245760
  122.8 5.8 %copy-start.4 = (u32[32]{0:T(128)S(1)}, u32[32]{0:T(128)}, u32[]{:S(2)}) copy-start(u32[32]{0:T(128)} %constant.6) | copy-start | bytes 388
  123.6 219.9 %reduce-scatter.38.cloned.1.call-start = ((), (), s32[]{:S(2)}) async-start(), calls=%async_computation.15 | async-start | bytes 245760
  124.5 241.3 %reduce-scatter.36.cloned.1.call-start = ((), (), s32[]{:S(2)}) async-start(), calls=%async_computation.14 | async-start | bytes 245760
  125.5 262.8 %reduce-scatter.34.cloned.1.call-start = ((), (), s32[]{:S(2)}) async-start(), calls=%async_computation.13 | async-start | bytes 245760
  126.3 284.1 %reduce-scatter.32.cloned.1.call-start = ((), (), s32[]{:S(2)}) async-start(), calls=%async_computation.12 | async-start | bytes 245760
  127.2 309.8 %reduce-scatter.44.cloned.1.call-start = ((), (), s32[]{:S(2)}) async-start(), calls=%async_computation.18 | async-start | bytes 983040
  128.5 426.5 %all-reduce.9.cloned.1.call-start = ((), (), s32[]{:S(2)}) async-start(), calls=%async_computation.21 | async-start | bytes 4919296 | tf_op jit(solution)/shard_map/psum | solution.py:596
  555.0 2.8 copy-start.1
  555.0 3.4 copy-start
Sparse Core Ops, SparseCore 0:
  119.5 33.4 all-reduce.6
  155.7 48.3 reduce-scatter.27
  206.7 47.8 reduce-scatter.29
  257.0 19.7 reduce-scatter.45
  279.2 19.7 reduce-scatter.41
  301.4 19.7 reduce-scatter.39
  323.8 19.7 reduce-scatter.37
  346.1 19.7 reduce-scatter.35
  368.5 19.7 reduce-scatter.33
  390.7 19.7 reduce-scatter.31
  413.7 23.2 reduce-scatter.43
  441.4 113.5 all-reduce.8

commit v3 on v2

--- a/solution.py
+++ b/solution.py
@@ -52,7 +52,7 @@
 
 
 class Sizes:
-    def __init__(self, parts, slots, patches, channels, hidden, layers):
+    def __init__(self, parts, copies, slots, patches, channels, hidden, layers):
         self.parts = parts
         self.slots = slots
         self.patches = patches
@@ -72,18 +72,45 @@
         self.pad = -(-self.mix_cols // 128) * 128
         self.left = -(-self.groups * self.mine // TILE) * TILE
         self.whole = parts * patches
+        self.quarters = hidden // channels
+        self.far = min(copies // 2, 4)
+        self.rest = copies // (2 * self.far)
+        cuts = 2 * self.far
+        step = TILE * cuts
+        tail = self.main + 2 * TILE
+        self.job_rows = [-(-count // step) * step for count in (channels, channels + tail)]
+        self.shares = [count // cuts for count in self.job_rows]
+        act_rows = 2 * self.quarters * self.rows * self.groups
+        at = (layers - 1) * act_rows
+        self.places = []
+        for layer in range(layers):
+            for kind in range(2):
+                count, share = self.job_rows[kind], self.shares[kind]
+                place = {}
+                for name, size in (
+                    ("pay", 4 * count),
+                    ("got_pair", 2 * count),
+                    ("got_near", count),
+                    ("got_far", (self.far - 1) * 2 * share),
+                    ("got_cross", share),
+                    ("got_rest", (self.rest - 1) * share),
+                    ("final", share),
+                ):
+                    place[name] = at
+                    at += size
+                self.places.append(place)
+        self.kept_rows = max(at, layers * act_rows)
 
 
 def whole_kernel(
     z,
-    keep,
     x_hbm, dy_hbm, mask_ref, mixw_ref, mixb_ref,
     mgain_ref, mshift_ref, mscale_ref, pgain_ref, pshift_ref, pscale_ref, downb_ref, upb_ref,
     up_hbm, down_hbm,
-    out_w, out_e, dx_w, dx_e, du_hbm, dd_hbm, dm_ref, dv_ref, dub_ref,
-    du_ref, dd_ref, stage, send_x, send_dy, sende_x, sende_dy, got_x, got_dy,
-    xs, firsts, dys, outs_left, out_left, act, slope, up_w, down_w, mix_m, mix_t,
-    load_sem, own_sem, send_sem, recv_sem, lsend_sem, lrecv_sem,
+    out_w, out_e, dx_w, dx_e, sum_d, sum_u,
+    du_ref, dd_ref, dm_ref, dv_ref, dub_ref, stage, send_x, send_dy, sende_x, sende_dy, got_x, got_dy,
+    xs, firsts, dys, outs_left, out_left, kept, up_w, down_w, mix_m, mix_t,
+    load_sem, own_sem, send_sem, recv_sem, lsend_sem, lrecv_sem, job_send, job_recv, free_sem,
 ):
     dp, me = lax.axis_index("dp"), lax.axis_index("mix")
     parts, groups, channels, hidden = z.parts, z.groups, z.channels, z.hidden
@@ -105,8 +132,18 @@
         copy.start()
 
     barrier = pltpu.get_barrier_semaphore()
-    for r in range(1, parts):
-        pl.semaphore_signal(barrier, inc=1, device_id=(dp, peers[r]), device_id_type=MESH)
+    near, upper_place = lax.rem(dp, 2), lax.div(dp, 2)
+    far, rest = lax.rem(upper_place, z.far), lax.div(upper_place, z.far)
+    row_peers = [(dp, peers[r]) for r in range(1, parts)]
+    near_peer = (dp + 1 - 2 * near, me)
+    far_places = [lax.rem(far + r, z.far) for r in range(z.far)]
+    far_peers = [((rest * z.far + far_places[r]) * 2 + near, me) for r in range(z.far)]
+    rest_peers = [
+        ((lax.rem(rest + r, z.rest) * z.far + far) * 2 + near, me) for r in range(z.rest)
+    ]
+    job_peers = row_peers + [near_peer] + far_peers[1:] + rest_peers[1:]
+    for peer in job_peers:
+        pl.semaphore_signal(barrier, inc=1, device_id=peer, device_id_type=MESH)
 
     swap = swap_matrix()
     swap_b = swap.astype(BF16)
@@ -137,7 +174,7 @@
         send[...] = dot(matrix.astype(BF16), last).astype(BF16).reshape(parts, z.left, channels)
 
     def exchange(k, g, send, target):
-        copies = [pltpu.make_async_copy(send.at[g, me], target.at[g, pl.ds(me * z.block, z.block)], own_sem.at[k, g])]
+        copies = [lambda: pltpu.make_async_copy(send.at[g, me], target.at[g, pl.ds(me * z.block, z.block)], own_sem.at[k, g])]
         for r in range(1, parts):
             copies.append(
                 pltpu.make_async_remote_copy(
@@ -157,7 +194,7 @@
         return source.at[g, pl.ds(d * z.block, z.block)]
 
     def exchange_back(k, g, source, target):
-        copies = [pltpu.make_async_copy(part_of(source, g, me), target.at[g, me], own_sem.at[k, g])]
+        copies = [lambda: pltpu.make_async_copy(part_of(source, g, me), target.at[g, me], own_sem.at[k, g])]
         for r in range(1, parts):
             copies.append(
                 pltpu.make_async_remote_copy(
@@ -172,7 +209,7 @@
         return copies
 
     def exchange_left(k, send, target):
-        copies = [pltpu.make_async_copy(send.at[me], target.at[me], lsend_sem.at[k, 0])]
+        copies = [lambda: pltpu.make_async_copy(send.at[me], target.at[me], lsend_sem.at[k, 0])]
         for r in range(1, parts):
             copies.append(
                 pltpu.make_async_remote_copy(
@@ -187,11 +224,12 @@
         return copies
 
     def start(copies):
-        for copy in copies:
+        copies[0]().start()
+        for copy in copies[1:]:
             copy.start()
 
     def arrive(copies):
-        copies[0].wait()
+        copies[0]().wait()
         for copy in copies[1:]:
             copy.wait_recv()
 
@@ -203,7 +241,7 @@
         loads[g].wait()
         convert(send_x, g, swap_b)
         if g == 0:
-            pl.semaphore_wait(barrier, parts - 1)
+            pl.semaphore_wait(barrier, len(job_peers))
         start(exchange(0, g, send_x, xs.at[0]))
     convert_left(sende_x, None)
     for copy in loads[groups:]:
@@ -305,57 +343,96 @@
         firsts[l, g, z.body :, :] = (left + scale * left_total).astype(BF16)
 
     chunk = 512 if hidden % 512 == 0 else 128
-
-    def slot_of(l, g):
-        return l * groups + g if keep else 0
-
-    def mlp_hidden(l, g, normed, at):
+    back_chunk = 512 if hidden % 512 == 0 else 128
+
+    def kept_at(l, which, g, quarter):
+        index = (l * 2 + which) * groups + g
+        start = (index * z.quarters + quarter) * z.rows
+        return start if isinstance(start, int) else pl.multiple_of(start, TILE)
+
+    def pieces_of(h, chunk):
+        pieces, at = [], h
+        while at < h + chunk:
+            quarter, lane = divmod(at, channels)
+            end = min(channels, lane + h + chunk - at)
+            pieces.append((quarter, lane, end))
+            at += end - lane
+        return pieces
+
+    def keep_rows(l, which, g, h, value, chunk, first):
+        value, at = value.astype(BF16), 0
+        for quarter, lane, end in pieces_of(h, chunk):
+            place = pl.ds(kept_at(l, which, g, quarter) + first, value.shape[0])
+            kept[place, lane:end] = value[:, at : at + end - lane]
+            at += end - lane
+
+    def kept_rows(l, which, g, h, chunk):
+        parts_ = [
+            kept[pl.ds(kept_at(l, which, g, quarter), z.rows), lane:end]
+            for quarter, lane, end in pieces_of(h, chunk)
+        ]
+        return jnp.concatenate(parts_, axis=1)
+
+    def mlp_hidden(l, g, normed, first):
         bias = upb_ref[l : l + 1, :].astype(F32)
         for h in range(0, hidden, chunk):
             value = dot(normed, up_w[l, :, h : h + chunk]) + bias[:, h : h + chunk]
             active, grade = gelu_pair(value)
             active = active.astype(BF16)
-            act[at, :, h : h + chunk] = active
-            slope[at, :, h : h + chunk] = grade.astype(BF16)
+            keep_rows(l, 0, g, h, active, chunk, first)
+            keep_rows(l, 1, g, h, grade, chunk, first)
             yield h, active
 
-    def mlp_normed(l, g):
-        rows = firsts[l, g].astype(F32)
+    def mlp_normed(l, g, span=slice(None)):
+        rows = firsts[l, g, span, :].astype(F32)
         return rows, (vector(pgain_ref, l) * rows + vector(pshift_ref, l)).astype(BF16)
 
+    middle = z.rows // 2 // TILE * TILE
+    spans = (slice(0, middle), slice(middle, z.rows))
+
     def mlp_forward(l, g, target):
+        for span in spans:
+            rows, normed = mlp_normed(l, g, span)
+            total = None
+            for h, active in mlp_hidden(l, g, normed, span.start):
+                term = dot(active, down_w[l, h : h + chunk, :])
+                total = term if total is None else total + term
+            result = rows + vector(pscale_ref, l) * (total + vector(downb_ref, l))
+            result = result.astype(BF16)
+            if target is not None:
+                target[g, span, :] = result
+                continue
+            if span.start == 0:
+                sent(exchange(0, g, send_x, xs.at[0]))
+            for d in range(parts):
+                low, high = max(span.start, d * z.block), min(span.stop, (d + 1) * z.block)
+                if low < high:
+                    send_x[g, d, low - d * z.block : high - d * z.block, :] = result[
+                        low - span.start : high - span.start
+                    ]
+            if span.stop == z.rows:
+                outs_left[g] = result[z.body - span.start :]
+
+    def mlp_backward_down(l, g):
+        branch = (vector(pscale_ref, l) * dys[g].astype(F32)).astype(BF16)
+        dv_ref[l, 5:6, :] += jnp.sum(branch.astype(F32), axis=0, keepdims=True)
+        branch_t = branch.T
+        for h in range(0, hidden, back_chunk):
+            span = slice(h, h + back_chunk)
+            dd_ref[:, span] += dot(branch_t, kept_rows(l, 0, g, h, back_chunk))
+
+    def mlp_backward_up(l, g):
         rows, normed = mlp_normed(l, g)
-        total = None
-        for h, active in mlp_hidden(l, g, normed, slot_of(l, g)):
-            term = dot(active, down_w[l, h : h + chunk, :])
-            total = term if total is None else total + term
-        result = rows + vector(pscale_ref, l) * (total + vector(downb_ref, l))
-        result = result.astype(BF16)
-        if target is not None:
-            target[g] = result
-        else:
-            sent(exchange(0, g, send_x, xs.at[0]))
-            send_x[g] = result[: z.body].reshape(parts, z.block, channels)
-            outs_left[g] = result[z.body :]
-
-    def mlp_backward(l, g):
-        rows, normed = mlp_normed(l, g)
-        at = slot_of(l, g)
-        if not keep:
-            for _ in mlp_hidden(l, g, normed, at):
-                pass
         upper = dys[g].astype(F32)
         branch = (vector(pscale_ref, l) * upper).astype(BF16)
-        dv_ref[l, 5:6, :] += jnp.sum(branch.astype(F32), axis=0, keepdims=True)
-        normed_t, branch_t = normed.T, branch.T
+        normed_t = normed.T
         total = None
-        for h in range(0, hidden, chunk):
-            span = slice(h, h + chunk)
+        for h in range(0, hidden, back_chunk):
+            span = slice(h, h + back_chunk)
             back = dot_nt(branch, down_w[l, span, :])
-            grad = (back * slope[at, :, span].astype(F32)).astype(BF16)
+            grad = (back * kept_rows(l, 1, g, h, back_chunk).astype(F32)).astype(BF16)
             dub_ref[l, :, span] += jnp.sum(grad.astype(F32), axis=0, keepdims=True)
             du_ref[:, span] += dot(normed_t, grad)
-            dd_ref[:, span] += dot(branch_t, act[at, :, span])
             term = dot_nt(grad, up_w[l, :, span])
             total = term if total is None else total + term
         dv_ref[l, 3:4, :] += jnp.sum(total * rows, axis=0, keepdims=True)
@@ -409,40 +486,268 @@
     arrive(exchange_left(1, sende_dy, got_dy))
     spread_left(got_dy, dys)
 
-    def backward(l):
-        def step(g, carry):
-            if l == z.layers - 1:
-                arrive(exchange(1, g, send_dy, dys))
-                start(exchange_back(2, g, send_x, out_w))
-            mlp_backward(l, g)
-            mix_backward(l, g, dys)
-            if l == 0:
-                start(exchange_back(3, g, dys, dx_w))
-            return carry
-
-        return step
-
-    for l in reversed(range(z.layers)):
-        for ref in (du_ref, dd_ref):
-            ref[...] = jnp.zeros(ref.shape, F32)
-        lax.fori_loop(0, groups, backward(l), 0)
-        if l == z.layers - 1:
-            start(exchange_left(2, out_left, out_e))
-
-        turned = dd_ref[...] * down_w[l].astype(F32).T
-        dv_ref[l, 6:7, :] = jnp.sum(turned, axis=1)[None, :]
-        dv_ref[l, 6:7, :] += vector(downb_ref, l) * dv_ref[l, 5:6, :]
-        dv_ref[l, 6:7, :] = dv_ref[l, 6:7, :] / vector(pscale_ref, l)
+    low, high = lax.rem(me, 2), lax.div(me, 2)
+    pair_peer = (dp, high * 2 + 1 - low)
+    cross_peer = (dp, (1 - high) * 2 + low)
+
+    def aligned(start):
+        return start if isinstance(start, int) else pl.multiple_of(start, TILE)
+
+    def span_of(start, count):
+        return pl.ds(aligned(start), count)
+
+    def remote(job, slot, source, target, peer):
+        return pltpu.make_async_remote_copy(
+            src_ref=source,
+            dst_ref=target,
+            send_sem=job_send.at[job, slot],
+            recv_sem=job_recv.at[job, slot],
+            device_id=peer,
+            device_id_type=MESH,
+        )
+
+    class Job:
+        def __init__(self, layer, kind):
+            self.layer, self.kind = layer, kind
+            self.number = layer * 2 + kind
+            self.rows, self.share = z.job_rows[kind], z.shares[kind]
+            self.place = z.places[self.number]
+            self.sums = (sum_d, sum_u)[kind].at[layer]
+            self.own = self.place["pay"] + low * 2 * self.rows
+            self.half = self.own + near * self.rows
+            self.mine = self.half + far * 2 * self.share
+
+        def fill(self, tile_of):
+            for chunk_ in range(parts):
+                for t in range(self.rows // TILE):
+                    k, inner = divmod(t * TILE, self.share)
+                    at = self.place["pay"] + (chunk_ % 2) * 2 * self.rows
+                    at += (k * 2 + chunk_ // 2) * self.share + inner
+                    value = tile_of(chunk_, t)
+                    if value is None:
+                        kept[at : at + TILE, :] = jnp.zeros((TILE, channels), BF16)
+                    else:
+                        kept[at : at + TILE, : value.shape[1]] = value.astype(BF16)
+                        if value.shape[1] < channels:
+                            rest = channels - value.shape[1]
+                            kept[at : at + TILE, value.shape[1] :] = jnp.zeros((TILE, rest), BF16)
+
+        def pair_copy(self):
+            source = kept.at[span_of(self.place["pay"] + (1 - low) * 2 * self.rows, 2 * self.rows)]
+            target = kept.at[span_of(self.place["got_pair"], 2 * self.rows)]
+            return remote(self.number, 0, source, target, pair_peer)
+
+        def near_copy(self):
+            source = kept.at[span_of(self.own + (1 - near) * self.rows, self.rows)]
+            target = kept.at[span_of(self.place["got_near"], self.rows)]
+            return remote(self.number, 1, source, target, near_peer)
+
+        def far_copy(self, r):
+            source = kept.at[span_of(self.half + far_places[r] * 2 * self.share, 2 * self.share)]
+            target = kept.at[span_of(self.place["got_far"] + (r - 1) * 2 * self.share, 2 * self.share)]
+            return remote(self.number, 3 + r, source, target, far_peers[r])
+
+        def cross_copy(self):
+            source = kept.at[span_of(self.mine + (1 - high) * self.share, self.share)]
+            target = kept.at[span_of(self.place["got_cross"], self.share)]
+            return remote(self.number, 2, source, target, cross_peer)
+
+        def place_of(self, near_, far_):
+            return self.sums.at[span_of((near_ * z.far + far_) * self.share, self.share)]
+
+        def share_copy(self, r):
+            source = kept.at[span_of(self.place["final"], self.share)]
+            return remote(self.number, 3 + z.far + r, source, self.place_of(near, far), far_peers[r])
+
+        def rest_copy(self, r):
+            source = kept.at[span_of(self.mine + high * self.share, self.share)]
+            target = kept.at[span_of(self.place["got_rest"] + (r - 1) * self.share, self.share)]
+            return remote(self.number, 3 + 2 * z.far + r, source, target, rest_peers[r])
+
+        def own_copy(self):
+            source = kept.at[span_of(self.place["final"], self.share)]
+            return pltpu.make_async_copy(source, self.place_of(near, far), own_sem.at[4, self.number])
+
+        def back_copy(self):
+            block = self.sums.at[span_of(near * z.far * self.share, z.far * self.share)]
+            return remote(self.number, 3, block, block, near_peer)
+
+        def add(self, start, count, *others):
+            for at in range(0, count, 8 * TILE):
+                size = min(8 * TILE, count - at)
+                total = kept[span_of(start + at, size), :].astype(F32)
+                for other in others:
+                    total += kept[span_of(other + at, size), :].astype(F32)
+                yield at, size, total.astype(BF16)
+
+        def step(self, number):
+            if number == 0:
+                self.pair_copy().start()
+            elif number == 1:
+                self.pair_copy().wait_recv()
+                for half in (1 - near, near):
+                    start = half * self.rows
+                    for at, size, total in self.add(
+                        self.own + start, self.rows, self.place["got_pair"] + start
+                    ):
+                        kept[span_of(self.own + start + at, size), :] = total
+                    if half is not near:
+                        self.near_copy().start()
+            elif number == 2:
+                self.near_copy().wait_recv()
+                for at, size, total in self.add(self.half, self.rows, self.place["got_near"]):
+                    kept[span_of(self.half + at, size), :] = total
+                for r in range(1, z.far):
+                    self.far_copy(r).start()
+            elif number == 3:
+                for r in range(1, z.far):
+                    self.far_copy(r).wait_recv()
+                others = [self.place["got_far"] + (r - 1) * 2 * self.share for r in range(1, z.far)]
+                for at, size, total in self.add(self.mine, 2 * self.share, *others):
+                    kept[span_of(self.mine + at, size), :] = total
+                self.cross_copy().start()
+            elif number == 4:
+                self.cross_copy().wait_recv()
+                start = self.mine + high * self.share
+                for at, size, total in self.add(start, self.share, self.place["got_cross"]):
+                    kept[span_of(start + at, size), :] = total
+                for r in range(1, z.rest):
+                    self.rest_copy(r).start()
+                for r in range(1, z.rest):
+                    self.rest_copy(r).wait_recv()
+                others = [self.place["got_rest"] + r * self.share for r in range(z.rest - 1)]
+                for at, size, total in self.add(start, self.share, *others):
+                    kept[span_of(self.place["final"] + at, size), :] = total
+                self.own_copy().start()
+                for r in range(1, z.far):
+                    self.share_copy(r).start()
+            elif number == 5:
+                self.own_copy().wait()
+                for r in range(1, z.far):
+                    self.share_copy(r).wait_recv()
+                self.back_copy().start()
+            else:
+                self.back_copy().wait()
+                self.pair_copy().wait_send()
+                self.near_copy().wait_send()
+                self.cross_copy().wait_send()
+                for r in range(1, z.far):
+                    self.far_copy(r).wait_send()
+                    self.share_copy(r).wait_send()
+                for r in range(1, z.rest):
+                    self.rest_copy(r).wait_send()
+
+    def chunk_lanes(ref, chunk_):
+        return slice(chunk_ * channels, (chunk_ + 1) * channels)
+
+    def down_tile(chunk_, t):
+        if t * TILE >= channels:
+            return None
+        return dd_ref[t * TILE : (t + 1) * TILE, chunk_lanes(dd_ref, chunk_)]
+
+    def up_tile(l):
+        def tile_of(chunk_, t):
+            at = t * TILE
+            if at < channels:
+                return du_ref[at : at + TILE, chunk_lanes(du_ref, chunk_)]
+            at -= channels
+            if at < z.main:
+                return dm_ref[l, chunk_ * z.main + at : chunk_ * z.main + at + TILE, :]
+            if at == z.main:
+                return dm_ref[l, z.image : z.image + TILE, :]
+            if at == z.main + TILE:
+                bias = dub_ref[l, :, chunk_lanes(dub_ref, chunk_)]
+                rows = [dv_ref[l, 0:7, :], bias, jnp.zeros((TILE - 8, channels), F32)]
+                return jnp.concatenate(rows, axis=0)
+            return None
+
+        return tile_of
+
+    def down_sums(l):
+        total = None
+        for h in range(0, hidden, 2 * 128):
+            span = slice(h, h + 2 * 128)
+            term = dd_ref[:, span].T * down_w[l, span, :].astype(F32)
+            total = term if total is None else total + term
+        total = jnp.sum(total, axis=0, keepdims=True) + vector(downb_ref, l) * dv_ref[l, 5:6, :]
+        dv_ref[l, 6:7, :] = total / vector(pscale_ref, l)
+
+    def mix_sums(l):
         total = vector(mgain_ref, l) * dv_ref[l, 0:1, :] + vector(mshift_ref, l) * dv_ref[l, 1:2, :]
         dv_ref[l, 2:3, :] = (total + dv_ref[l, 2:3, :]) / vector(mscale_ref, l)
-        keeps = [
-            pltpu.make_async_copy(du_ref, du_hbm.at[l], load_sem.at[0]),
-            pltpu.make_async_copy(dd_ref, dd_hbm.at[l], load_sem.at[1]),
-        ]
-        for copy in keeps:
-            copy.start()
-        for copy in keeps:
-            copy.wait()
+
+    jobs = {(l, kind): Job(l, kind) for l in range(z.layers) for kind in range(2)}
+    top = z.layers - 1
+
+    def clear(*refs):
+        for ref in refs:
+            ref[...] = jnp.zeros(ref.shape, F32)
+
+    def backward_top(g, carry):
+        arrive(exchange(1, g, send_dy, dys))
+        start(exchange_back(2, g, send_x, out_w))
+        mlp_backward_down(top, g)
+        mlp_backward_up(top, g)
+        mix_backward(top, g, dys)
+        return carry
+
+    clear(du_ref, dd_ref)
+    lax.fori_loop(0, groups, backward_top, 0)
+    start(exchange_left(2, out_left, out_e))
+    for peer in job_peers:
+        pl.semaphore_signal(free_sem, inc=1, device_id=peer, device_id_type=MESH)
+    down_sums(top)
+    mix_sums(top)
+    jobs[top, 0].fill(down_tile)
+    jobs[top, 1].fill(up_tile(top))
+    pl.semaphore_wait(free_sem, len(job_peers))
+    jobs[top, 0].step(0)
+    jobs[top, 1].step(0)
+
+    def backward_down(l):
+        def step(g, carry):
+            mlp_backward_down(l, g)
+            return carry
+
+        return step
+
+    def backward_up(l, g):
+        mlp_backward_up(l, g)
+        mix_backward(l, g, dys)
+        if l == 0:
+            start(exchange_back(3, g, dys, dx_w))
+
+    plan = {
+        (0, 0): [(top, 0, 1), (top, 1, 1)],
+        (0, 1): [(top, 0, 2), (0, 0, 1)],
+        (0, 2): [(top, 1, 2), (top, 0, 3)],
+        (0, 3): [(0, 0, 2), (top, 0, 4), (top, 1, 3)],
+        (0, 4): [(0, 1, 1), (top, 1, 4), (0, 0, 3), (top, 0, 5), (0, 1, 2), (0, 0, 4), (top, 1, 5), (0, 1, 3), (0, 0, 5),
+                 (0, 1, 4), (0, 1, 5), (top, 0, 6), (top, 1, 6), (0, 0, 6), (0, 1, 6)],
+    }
+
+    def run(point):
+        for l, kind, number in plan.get(point, ()):
+            jobs[l, kind].step(number)
+
+    clear(du_ref, dd_ref)
+    lax.fori_loop(0, groups, backward_down(0), 0)
+    run((0, 0))
+    down_sums(0)
+    jobs[0, 0].fill(down_tile)
+    jobs[0, 0].step(0)
+    thirds = [groups * k // 3 for k in range(4)]
+    for k in range(3):
+        def step(g, carry):
+            backward_up(0, g)
+            return carry
+
+        lax.fori_loop(thirds[k], thirds[k + 1], step, 0)
+        run((0, k + 1))
+    mix_sums(0)
+    jobs[0, 1].fill(up_tile(0))
+    jobs[0, 1].step(0)
+    run((0, 4))
 
     for g in range(groups):
         sent(exchange(1, g, send_dy, dys))
@@ -460,7 +765,11 @@
             sent(copies)
 
 
-def finish_kernel(z, mask_ref, out_w, out_e, dx_w, dx_e, out_ref, dx_ref):
+def finish_kernel(
+    z, mask_ref, out_w, out_e, dx_w, dx_e, sum_d, sum_u,
+    out_ref, dx_ref, gain_ref, shift_ref, scale_ref, mixw_ref, mixb_ref, pgain_ref, pshift_ref, pscale_ref,
+    up_ref, upb_ref, down_ref, downb_ref,
+):
     g = pl.program_id(0)
     swap = swap_matrix()
     pick = iota((1, GROUP * TILE), 1) >> 4
@@ -492,13 +801,55 @@
         target[z.patches - 1] = rows.astype(target.dtype)
 
 
-def local(parts, images_in, out_grad, slot_mask, mix_gain, mix_shift, mix_scale, mix_weight, mix_bias,
+    @pl.when(g == 0)
+    def _():
+        me = lax.axis_index("mix")
+        channels, share = z.channels, z.channels // z.parts
+        row, lane = iota((z.pad, z.whole), 0), iota((z.pad, z.whole), 1)
+        want = row
+        for m in range(1, z.parts):
+            want = want + jnp.where(row >= m * z.main, 1, 0)
+        for m in range(z.parts):
+            base = z.image + m * z.mine
+            inside = (row >= base) & (row < base + z.mine)
+            want = jnp.where(inside, m * z.patches + z.patches - 1, want)
+        want = jnp.where(row < z.mix_rows, want, -1)
+        order = jnp.where(want == lane, 1.0, 0.0).astype(BF16)
+        lanes_in, lanes_out = iota((channels, share), 0), iota((channels, share), 1)
+        own = jnp.where(lanes_in == lanes_out + me * share, 1.0, 0.0).astype(BF16)
+        size = z.main + TILE
+        at = iota((size, 1), 0) - z.main - me * z.mine
+        edge = jnp.where((at >= 0) & (at < z.mine), 1.0, 0.0)
+        fold_row, fold_lane = iota((size, z.patches), 0), iota((size, z.patches), 1)
+        fold_at = fold_row - z.main - me * z.mine
+        fold_to = jnp.where(
+            fold_row < z.main, fold_row, jnp.where((fold_at >= 0) & (fold_at < z.mine), z.main, -1)
+        )
+        fold = jnp.where(fold_to == fold_lane, 1.0, 0.0).astype(BF16)
+        spot = jnp.where((iota((8, z.pad), 0) == 0) & (iota((8, z.pad), 1) == z.ones), 1.0, 0.0)
+        for l in range(z.layers):
+            up_ref[l] = sum_u[l, :channels, :].astype(F32)
+            down_ref[l] = sum_d[l, :channels, :].astype(F32).T
+            rows = sum_u[l, channels : channels + size, : z.pad]
+            weight = dot(rows, order)
+            mixw_ref[: z.main, l, :] = weight[: z.main]
+            mixw_ref[z.main, l : l + 1, :] = jnp.sum(weight * edge, axis=0, keepdims=True)
+            bias = dot_nt(spot.astype(BF16), rows).astype(BF16)
+            mixb_ref[l : l + 1, :] = dot(bias, fold)[:1]
+            tile = sum_u[l, channels + size : channels + size + TILE, :]
+            vectors = dot(tile, own)
+            for k, ref in enumerate(
+                (gain_ref, shift_ref, scale_ref, pgain_ref, pshift_ref, downb_ref, pscale_ref)
+            ):
+                ref[l : l + 1, :] = vectors[k : k + 1]
+            upb_ref[l : l + 1, :] = tile[7:8, :].astype(F32)
+
+
+def local(parts, copies, images_in, out_grad, slot_mask, mix_gain, mix_shift, mix_scale, mix_weight, mix_bias,
           mlp_gain, mlp_shift, mlp_scale, up_weight, up_bias, down_weight, down_bias):
     slots, patches, channels = images_in.shape
     layers, _, hidden = up_weight.shape
-    z = Sizes(parts, slots, patches, channels, hidden, layers)
-    keep = layers * z.groups * z.rows * hidden * 4 <= 30e6
-    kept = layers * z.groups if keep else 1
+    z = Sizes(parts, copies, slots, patches, channels, hidden, layers)
     vmem = pl.BlockSpec(memory_space=pltpu.VMEM)
     smem = pl.BlockSpec(memory_space=pltpu.SMEM)
     hbm = pl.BlockSpec(memory_space=pl.ANY)
@@ -506,21 +857,21 @@
     left = jax.ShapeDtypeStruct((parts, z.left, channels), BF16)
     dma = pltpu.SemaphoreType.DMA
     rows = (z.groups, z.rows, channels)
-    out_w, out_e, dx_w, dx_e, du, dd, dm, dv, dub = pl.pallas_call(
-        functools.partial(whole_kernel, z, keep),
+    out_w, out_e, dx_w, dx_e, sum_d, sum_u = pl.pallas_call(
+        functools.partial(whole_kernel, z),
         out_shape=(
             wire, left, wire, left,
-            jax.ShapeDtypeStruct((layers, channels, hidden), F32),
-            jax.ShapeDtypeStruct((layers, channels, hidden), F32),
-            jax.ShapeDtypeStruct((layers, z.pad, z.pad), F32),
-            jax.ShapeDtypeStruct((layers, 8, channels), F32),
-            jax.ShapeDtypeStruct((layers, 1, hidden), F32),
+            jax.ShapeDtypeStruct((layers, z.job_rows[0], channels), BF16),
+            jax.ShapeDtypeStruct((layers, z.job_rows[1], channels), BF16),
         ),
         in_specs=[hbm, hbm, smem] + [vmem] * 10 + [hbm, hbm],
-        out_specs=(hbm,) * 6 + (vmem,) * 3,
+        out_specs=(hbm,) * 6,
         scratch_shapes=[
             pltpu.VMEM((channels, hidden), F32),
             pltpu.VMEM((channels, hidden), F32),
+            pltpu.VMEM((layers, z.pad, z.pad), F32),
+            pltpu.VMEM((layers, 8, channels), F32),
+            pltpu.VMEM((layers, 1, hidden), F32),
             pltpu.VMEM((z.groups, patches, GROUP, channels), BF16),
             pltpu.VMEM((z.groups, parts, z.block, channels), BF16),
             pltpu.VMEM((z.groups, parts, z.block, channels), BF16),
@@ -533,18 +884,20 @@
             pltpu.VMEM(rows, BF16),
             pltpu.VMEM((z.groups, parts * z.mine, channels), BF16),
             pltpu.VMEM((parts, z.left, channels), BF16),
-            pltpu.VMEM((kept, z.rows, hidden), BF16),
-            pltpu.VMEM((kept, z.rows, hidden), BF16),
+            pltpu.VMEM((z.kept_rows, channels), BF16),
             pltpu.VMEM((layers, channels, hidden), BF16),
             pltpu.VMEM((layers, hidden, channels), BF16),
             pltpu.VMEM((layers, z.pad, z.pad), BF16),
             pltpu.VMEM((layers, z.pad, z.pad), BF16),
             dma((2 * z.groups + 2,)),
-            dma((4, z.groups)),
+            dma((5, max(z.groups, 2 * layers))),
             dma((4, z.groups, parts)),
             dma((4, z.groups, parts)),
             dma((4, parts)),
             dma((4, parts)),
+            dma((2 * layers, 3 + 2 * z.far + z.rest)),
+            dma((2 * layers, 3 + 2 * z.far + z.rest)),
+            pltpu.SemaphoreType.REGULAR,
         ],
         compiler_params=pltpu.CompilerParams(
             collective_id=0, has_side_effects=True, vmem_limit_bytes=64 << 20
@@ -563,39 +916,40 @@
     block = pl.BlockSpec((1, *flat[1:]), lambda g: (g, 0, 0))
     whole = pl.BlockSpec(left.shape, lambda g: (0, 0, 0))
     turned = pl.BlockSpec((patches, GROUP, channels), lambda g: (0, g, 0))
-    output, input_grad = pl.pallas_call(
-        functools.partial(finish_kernel, z),
-        grid=(z.groups,),
-        out_shape=(
-            jax.ShapeDtypeStruct((patches, slots, channels), BF16),
-            jax.ShapeDtypeStruct((patches, slots, channels), F32),
-        ),
-        in_specs=[smem, block, whole, block, whole],
-        out_specs=(turned, turned),
-        name="finish",
-    )(slot_mask, out_w.reshape(flat), out_e, dx_w.reshape(flat), dx_e)
-    output = jnp.transpose(output, (1, 0, 2))
-    input_grad = jnp.transpose(input_grad, (1, 0, 2))
-
-    main = dm[:, : z.image, : z.image].reshape(layers, parts, z.main, parts, z.main)
-    edge_q = dm[:, : z.image, z.image : z.mix_rows].reshape(layers, parts, z.main, parts, z.mine).sum(-1)
-    edge_p = dm[:, z.image : z.mix_rows, : z.image].reshape(layers, parts, z.mine, parts, z.main).sum(2)
-    corner = dm[:, z.image : z.mix_rows, z.image : z.mix_rows].reshape(layers, parts, z.mine, parts, z.mine).sum((2, 4))
-    top = jnp.concatenate([main, edge_q[..., None]], axis=-1)
-    low = jnp.concatenate([edge_p, corner[..., None]], axis=-1)
-    weight = jnp.concatenate([top, low[:, :, None]], axis=2).reshape(layers, z.whole, z.whole)
-    bias_main = dm[:, : z.image, z.ones].reshape(layers, parts, z.main)
-    bias_edge = dm[:, z.image : z.mix_rows, z.ones].reshape(layers, parts, z.mine).sum(-1)
-    bias = jnp.concatenate([bias_main, bias_edge[..., None]], axis=-1).reshape(layers, z.whole)
-    shares = [dv[:, 0], dv[:, 1], dv[:, 2], weight, bias, dv[:, 3], dv[:, 4], dv[:, 6], du, dub[:, 0], dd, dv[:, 5]]
-    axes = [1, 1, 1, 1, 1, 1, 1, 1, 2, 1, 2, 1]
-    shares = tuple(
-        lax.psum_scatter(share, "mix", scatter_dimension=axis, tiled=True)
-        for share, axis in zip(shares, axes)
+    share = channels // parts
+    small = jax.ShapeDtypeStruct((layers, share), F32)
+    small_block = pl.BlockSpec(small.shape, lambda g: (0, 0))
+    shapes = [
+        jax.ShapeDtypeStruct((patches, slots, channels), BF16),
+        jax.ShapeDtypeStruct((patches, slots, channels), F32),
+        small, small, small,
+        jax.ShapeDtypeStruct((patches, layers, z.whole), F32),
+        jax.ShapeDtypeStruct((layers, patches), F32),
+        small, small, small,
+        jax.ShapeDtypeStruct((layers, channels, hidden // parts), F32),
+        jax.ShapeDtypeStruct((layers, hidden // parts), F32),
+        jax.ShapeDtypeStruct((layers, hidden // parts, channels), F32),
+        small,
+    ]
+
+    def fixed(shape):
+        return pl.BlockSpec(shape, lambda g: (0,) * len(shape))
+
+    sums = [fixed(sum_d.shape), fixed(sum_u.shape)]
+    results = list(
+        pl.pallas_call(
+            functools.partial(finish_kernel, z),
+            grid=(z.groups,),
+            out_shape=shapes,
+            in_specs=[smem, block, whole, block, whole] + sums,
+            out_specs=[turned, turned] + [fixed(shape.shape) for shape in shapes[2:]],
+            compiler_params=pltpu.CompilerParams(vmem_limit_bytes=48 << 20),
+            name="finish",
+        )(slot_mask, out_w.reshape(flat), out_e, dx_w.reshape(flat), dx_e, sum_d, sum_u)
     )
-    grads = list(lax.psum(shares, "dp"))
-    grads[10] = jnp.swapaxes(grads[10], 1, 2)
-    return (output, input_grad, *grads)
+    for k in (0, 1, 5):
+        results[k] = jnp.transpose(results[k], (1, 0, 2))
+    return tuple(results)
 
 
 def solution(mesh):
@@ -617,7 +971,7 @@
         P(None, "mix"),
     )
     return jax.shard_map(
-        functools.partial(local, mesh.shape["mix"]),
+        functools.partial(local, mesh.shape["mix"], mesh.shape["dp"]),
         mesh=mesh,
         in_specs=in_specs,
         out_specs=out_specs,

time: 567 us -> 180 us (0.32)
  waiting for transfers between devices: 365 us -> 0 us
  Pallas kernels: 111 us -> 169 us
  blocking collectives: 44.8 us -> 0 us
  local copies, waits for them, and re-layouts: 29.3 us -> 7.39 us
  between operations: 15 us -> 0.96 us
    unnamed x21 -> x0, waiting for transfers between devices: 187 us -> none
    reduce_scatter x2 -> x0, waiting for transfers between devices: 100 us -> none  [local(): lax.psum_scatter(share, 'mix', scatter_dimension=axis, tiled=True)]
    psum x1 -> x0, waiting for transfers between devices: 77.9 us -> none  [local(): grads = list(lax.psum(shares, 'dp'))]
    pallas_call x1, Pallas kernels: 105 us -> 163 us  [local(): pl.pallas_call(functools.partial(whole_kernel, z), out_shape=(wire, left,...]
    psum x1 -> x0, blocking collectives: 39 us -> none  [local(): grads = list(lax.psum(shares, 'dp'))]
    unnamed x32 -> x14, local copies, waits for them, and re-layouts: 20.6 us -> 7.39 us
    slice x8 -> x0, local copies, waits for them, and re-layouts: 5.8 us -> none  [the longest x1 1.18 us: local(): bias_main = dm[:, :z.image, z.ones].reshape(layers, parts, z.main)]
    unnamed x1 -> x0, blocking collectives: 5.74 us -> none
  transfers between devices with their start and end apart: 12 -> 0, of which waited for: 12 -> 0; matrix products, arithmetic and copies ran while one was open for 3% -> 0% of each run, Pallas kernels for 1% -> 0%
where the time goes in v3:
time: 180 us; the launch traced here: 177 us
  Pallas kernels  169 us (94%)
  local copies, waits for them, and re-layouts  7.39 us (4%)
    pallas_call x1, Pallas kernels, local(): pl.pallas_call(functools.partial(whole_kernel, z), out_shape=(wire, left,...  163 us
    unnamed x14, local copies, waits for them, and re-layouts  7.39 us
    pallas_call x1, Pallas kernels, local(): pl.pallas_call(functools.partial(finish_kernel, z), grid=(z.groups,), out...  5.37 us

profile of v3, /device:TPU:0, one launch (start us, length us, event | category | flops | bytes accessed | tf_op | source)
XLA Modules:
  0.0 177.0 jit_solution(9592814929135262361)
XLA Ops:
  0.7 163.3 %layers.1 = (bf16[3,4,192,384]{3,2,1,0:T(8,128)(2,1)}, bf16[4,16,384]{2,1,0:T(8,128)(2,1)}, bf16[3,4,192,384]{3,2,1,0:T(8,128)(2,1)}, bf16[4,16,384]{2,1,0:T(8,1...) custom-call(bf16[49,48,384]{2,1,0:T(8,128)(2,1)} %bitcast.10, bf16[49,48,384]{2,1,0:T(8,128)(2,1)} %bitcast.11, ...), custom_call_target="tpu_custom_call" | custom-call | tf_op jit(solution)/shard_map/layers/pallas_call | solution.py:860
  164.0 0.0 copy-start
  164.0 1.5 copy-done
  165.4 0.0 copy-start.1
  165.4 1.5 copy-done.1
  166.9 0.0 copy-start.2
  166.9 1.1 copy-done.2
  168.1 0.0 copy-start.3
  168.1 1.1 copy-done.3
  169.1 0.0 copy-start.4
  169.1 0.8 copy-done.4
  169.9 0.0 copy-start.5
  169.9 0.8 copy-done.5
  170.7 0.0 copy-start.6
  170.7 0.7 copy-done.6
  171.4 5.4 %finish.1 = (bf16[49,48,384]{2,1,0:T(8,128)(2,1)}, f32[49,48,384]{2,1,0:T(8,128)}, f32[2,96]{1,0:T(2,128)}, f32[2,96]{1,0:T(2,128)}, f32[2,96]{1,0:T(2,128)}, /*...) custom-call(s32[48]{0:T(128)S(1)} %copy-done.6, ...), custom_call_target="tpu_custom_call" | custom-call | tf_op jit(solution)/shard_map/finish/pallas_call | solution.py:940
Async XLA Ops:
  164.0 1.5 copy-start
  165.4 1.5 copy-start.1
  166.9 1.1 copy-start.2
  168.1 1.1 copy-start.3
  169.1 0.8 copy-start.4
  169.9 0.8 copy-start.5
  170.7 0.7 copy-start.6
